TPU v7x, 256 devices: a whole 4x4x8 slice. The times are simulated.
256 devices in a mesh: sx: 32 (over x, z_lo, core), sy: 8 (over z_hi, y).
Axes of the slice: x: 4, y: 4, z: 8 (z_hi: 2, z_lo: 4; z = z_hi * 4 + z_lo), core: 2. Of those that a mesh axis runs over, the one named last changes fastest.
Arguments:
- queries: bfloat16 [128, 5120], P('sx'), may hold values from -120 to 120
- cached_key_rows: bfloat16 [524288, 1024], P(('sx', 'sy')), may hold values from -6 to 6
- cached_value_rows: bfloat16 [524288, 1024], P(('sx', 'sy')), may hold values from -6 to 6
- stretch_opening_index: int32 [1], replicated, may hold values from 516096 to 524160
- valid_lengths: int32 [256], P(('sx', 'sy')), may hold values from 1024 to 2048, as said below
- out_weight: bfloat16 [5120, 5120], P('sy', 'sx'), may hold values from -0.078125 to 0.078125
Outputs:
- output: bfloat16 [128, 5120], P('sy', 'sx')
Inputs may be any that keep to these rules, and one draw needn't show every extreme that they name: `valid_lengths`: some block is full in every draw.
All inputs are finite; a program needn't handle non-finite values.
Results may differ from a plain program's by a relative error of at most 0.0049.
Values may be sent and summed in bfloat16 or wider, within the bound.
No kernel may reach another device: no remote copies, remote signals or barrier semaphores. Data moves between devices by JAX's collectives and lax.ppermute only.
A program may use at most 128 MiB of HBM per device.

v0:
```python
import jax
import jax.numpy as jnp
from jax import lax
from jax.sharding import PartitionSpec as P

HQ = 40
KEY_VALUE_HEADS = 8
HEAD_SIZE = 128
QUERY_GROUP_SIZE = 5


def normalizer_divisor(stretch_opening_index, number_entries_sequence):
    positions = stretch_opening_index[0] + jnp.arange(number_entries_sequence, dtype=jnp.int32)
    buckets = ((positions + 1) // 8192).astype(jnp.float32)
    return (1.0 + 0.1 * jnp.log(buckets + 1.0)) * HEAD_SIZE ** (-0.5)


def attend_head(
    all_queries, cached_key_rows, cached_value_rows, visible, score_multiplier, key_value_head
):
    number_entries_sequence = all_queries.shape[0]
    width = QUERY_GROUP_SIZE * HEAD_SIZE
    query_rows = all_queries[:, key_value_head * width : (key_value_head + 1) * width].reshape(
        number_entries_sequence * QUERY_GROUP_SIZE, HEAD_SIZE
    )
    key_block = cached_key_rows[:, key_value_head * HEAD_SIZE : (key_value_head + 1) * HEAD_SIZE]
    value_block = cached_value_rows[
        :, key_value_head * HEAD_SIZE : (key_value_head + 1) * HEAD_SIZE
    ]
    scores = lax.dot_general(
        query_rows, key_block, (((1,), (1,)), ((), ())), preferred_element_type=jnp.float32
    )
    scores = (
        scores.reshape(number_entries_sequence, QUERY_GROUP_SIZE, -1)
        * score_multiplier[:, None, None]
    )
    seen_mask = visible[:, None, :]
    scores = jnp.where(seen_mask, scores, -1e30)
    maxima = jnp.max(scores, axis=-1)
    weights = jnp.where(seen_mask, jnp.exp(scores - maxima[..., None]), 0.0)
    totals = jnp.sum(weights, axis=-1)
    rounded = weights.astype(jnp.bfloat16).reshape(number_entries_sequence * QUERY_GROUP_SIZE, -1)
    partial_value = jnp.dot(rounded, value_block, preferred_element_type=jnp.float32)
    return (partial_value.reshape(number_entries_sequence, width), maxima, totals)


def per_device(
    queries, cached_key_rows, cached_value_rows, stretch_opening_index, valid_lengths, out_weight
):
    all_queries = lax.all_gather(queries, "sx", axis=0, tiled=True)
    number_entries_sequence = all_queries.shape[0]
    slot_count = cached_key_rows.shape[0]
    leading_extent = lax.axis_size("sx")
    inner_size = lax.axis_size("sy")
    device_block = lax.axis_index("sx") * inner_size + lax.axis_index("sy")
    score_multiplier = normalizer_divisor(stretch_opening_index, number_entries_sequence)
    query_positions = stretch_opening_index[0] + jnp.arange(
        number_entries_sequence, dtype=jnp.int32
    )
    entry_indices = jnp.arange(slot_count, dtype=jnp.int32)
    key_positions = device_block * slot_count + entry_indices
    visible = (entry_indices < valid_lengths[0])[None, :] & (
        key_positions[None, :] <= query_positions[:, None]
    )
    partials = []
    maxima_list = []
    totals_list = []
    for key_value_head in range(KEY_VALUE_HEADS):
        partial_value, maxima, totals = attend_head(
            all_queries,
            cached_key_rows,
            cached_value_rows,
            visible,
            score_multiplier,
            key_value_head,
        )
        partials.append(partial_value)
        maxima_list.append(maxima)
        totals_list.append(totals)
    block_out = jnp.concatenate(partials, axis=1)
    block_max = jnp.concatenate(maxima_list, axis=1)
    block_total = jnp.concatenate(totals_list, axis=1)
    row_max = lax.pmax(block_max, ("sx", "sy"))
    factor = jnp.exp(block_max - row_max)
    scaled_out = (
        block_out.reshape(number_entries_sequence, HQ, HEAD_SIZE) * factor[..., None]
    ).reshape(number_entries_sequence, HQ * HEAD_SIZE)
    scaled_total = block_total * factor
    token_block = number_entries_sequence // leading_extent
    head_group = HQ // inner_size
    token_out, token_total = (
        lax.psum_scatter(scaled_out, "sx", scatter_dimension=0, tiled=True),
        lax.psum_scatter(scaled_total, "sx", scatter_dimension=0, tiled=True),
    )
    mine_out, mine_total = (
        lax.psum_scatter(token_out, "sy", scatter_dimension=1, tiled=True),
        lax.psum_scatter(token_total, "sy", scatter_dimension=1, tiled=True),
    )
    attended = mine_out.reshape(token_block, head_group, HEAD_SIZE) / mine_total[..., None]
    attended = attended.reshape(token_block, head_group * HEAD_SIZE).astype(jnp.bfloat16)
    gathered = lax.all_gather(attended, "sx", axis=0, tiled=True)
    summed = lax.psum_scatter(
        jnp.dot(gathered, out_weight, preferred_element_type=jnp.float32),
        "sy",
        scatter_dimension=0,
        tiled=True,
    )
    return summed.astype(jnp.bfloat16)


def solution(mesh):
    return jax.shard_map(
        per_device,
        mesh=mesh,
        in_specs=(
            P("sx", None),
            P(("sx", "sy"), None),
            P(("sx", "sy"), None),
            P(),
            P(("sx", "sy")),
            P("sy", "sx"),
        ),
        out_specs=P("sy", "sx"),
        check_vma=False,
    )
```

profile of v0, /device:TPU:1, one launch (start us, length us, event | category | flops | bytes accessed | tf_op | source)
XLA Modules:
  0.0 761.0 jit_solution(11848049618558348533)
XLA Ops:
  6.5 0.7 all-gather.4.cloned.1.call-update
  7.3 0.0 all-reduce.5.cloned.1.call-start
  8.7 0.2 compare_and_fusion
  8.9 63.9 %all-gather.4.cloned.1.call-done = bf16[32,4,5120]{2,1,0:T(4,128)(2,1)} async-done(((bf16[1,4,5120]{2,1,0:T(4,128)(2,1)}), bf16[32,4,5120]{2,1,0:T(4,128)(2,1)}) %all-gather.4.cloned.1.call-update) | async-done | bytes 1310736 | tf_op jit(solution)/shard_map/all_gather | solution.py:50
  72.8 2.5 reshape.172
  75.3 0.1 fusion.131
  75.4 0.2 copy.60
  75.6 0.2 copy.81
  75.8 0.2 copy.66
  76.0 4.2 fusion.94
  80.2 4.3 fusion.90
  84.5 0.2 copy.69
  84.7 4.3 fusion.88
  88.9 0.2 copy.72
  89.1 4.2 fusion.86
  93.3 0.2 copy.75
  93.4 4.3 fusion.84
  97.7 0.2 copy.78
  97.9 4.4 fusion.82
  102.3 0.2 copy.63
  102.5 6.8 fusion.7
  109.2 5.0 fusion.48
  114.2 16.3 %fusion.22 = (f32[128,5]{0,1:T(8,128)S(1)}, f32[128,5]{0,1:T(8,128)S(1)}, f32[128,5]{0,1:T(8,128)S(1)}, f32[128,5]{0,1:T(8,128)S(1)}, f32[128,5]{0,1:T(8,128)S(1...) fusion(f32[128,5,2048]{2,0,1:T(8,128)} %get-tuple-element.31, ...), kind=kOutput, calls=%fused_computation.38 | convolution fusion | flops 372239360 | bytes 42919424 | tf_op jit(solution)/shard_map/dot_general | solution.py:30
  130.5 0.4 concatenate.11
  130.9 0.0 copy-start.2
  130.9 15.7 %fusion.20 = (f32[128,5]{0,1:T(8,128)S(1)}, f32[128,5]{0,1:T(8,128)S(1)}, f32[128,5]{0,1:T(8,128)S(1)}, f32[128,5]{0,1:T(8,128)S(1)}, f32[128,5]{0,1:T(8,128)S(1)}, /*index=5*/f32[128,5]{0,1:T(8,128)S(1)}) fusion(f32[128,5,2048]{2,0,1:T(8,128)} %fusion.82, f32[128,5]{0,1:T(8,128)S(1)} %get-tuple-element.11, f32[128]{0:T(128)S(1)} %add_multiply_fusion, ...), kind=kLoop, calls=%fused_computation.36 | loop fusion | flops 39317760 | bytes 31750656 | tf_op jit(solution)/shard_map/reduce_sum | solution.py:41
  146.6 0.0 slice-start.2
  146.6 2.5 fusion.51
  149.0 5.0 fusion.54
  154.1 0.0 slice-start.6
  154.1 2.5 fusion.57
  156.6 0.0 slice-start.8
  156.6 2.5 fusion.60
  159.1 0.0 slice-start.10
  159.1 2.5 fusion.63
  161.6 2.5 fusion.66
  164.1 2.5 fusion.69
  166.6 76.6 %pmax.7 = f32[128,40]{0,1:T(8,128)S(1)} all-reduce(f32[128,40]{0,1:T(8,128)S(1)} %concatenate.11), channel_id=1, replica_groups=mesh['sx'=32,'sy'=8] {'sx','sy'}, use_global_device_ids=true, to_apply=%region_8.9 | all-reduce | flops 5120 | bytes 40960 | tf_op jit(solution)/shard_map/pmax | solution.py:83
  243.2 0.3 concatenate.12
  243.5 2.0 broadcast_multiply_fusion
  245.5 0.0 copy-start.4
  245.5 0.0 copy-start.3
  245.5 2.1 copy.84
  247.6 0.0 all-reduce.5.cloned.1.call-update
  247.7 0.0 reduce-scatter.8.cloned.1.call-start
  247.7 0.6 dynamic-slice
  248.3 0.6 dynamic-slice.4
  250.2 130.5 %all-reduce.1 = f32[128,40]{0,1:T(8,128)S(1)} all-reduce(f32[128,40]{0,1:T(8,128)S(1)} %get-tuple-element.21), channel_id=4, replica_groups=mesh['sx'=32,'sy'=8] {'sx'}, use_global_device_ids=true, to_apply=%region_19.20.clone | all-reduce | flops 5120 | bytes 40960
  380.8 0.1 constant_dynamic-slice_fusion.1
  380.8 41.2 %all-reduce.2 = f32[4,40]{0,1:T(8,128)S(1)} all-reduce(f32[4,40]{0,1:T(8,128)S(1)} %constant_dynamic-slice_fusion.1), channel_id=5, replica_groups=mesh['sx'=32,'sy'=8] {'sy'}, use_global_device_ids=true, to_apply=%region_20.21.clone | all-reduce | flops 160 | bytes 1280
  422.0 0.1 copy.85
  422.1 106.2 %all-reduce.5.cloned.1.call-done = f32[128,5120]{1,0:T(8,128)} async-done(((f32[128,5120]{1,0:T(8,128)}), f32[128,5120]{1,0:T(8,128)}) %all-reduce.5.cloned.1.call-update) | async-done | bytes 2621456
  528.3 0.9 constant_dynamic-slice_fusion.2
  529.3 2.3 copy.94
  531.6 0.0 reduce-scatter.8.cloned.1.call-update
  531.6 0.0 reduce-scatter.6.cloned.1.call-start
  531.6 0.1 broadcast_bitcast_fusion
  531.7 101.6 %reduce-scatter.8.cloned.1.call-done = f32[640,4]{1,0:T(8,128)} async-done(((f32[5120,4]{1,0:T(8,128)}), f32[640,4]{1,0:T(8,128)}) %reduce-scatter.8.cloned.1.call-update) | async-done | bytes 10256
  633.3 1.1 copy.95
  634.4 43.2 %all-gather.1 = bf16[32,4,640]{2,1,0:T(4,128)(2,1)S(1)} all-gather(bf16[1,4,640]{2,1,0:T(4,128)(2,1)S(1)} %fusion.113), channel_id=1, replica_groups=mesh['sx'=32,'sy'=8] {'sx'}, dimensions={0}, use_global_device_ids=true | all-gather | bytes 168960 | tf_op jit(solution)/shard_map/all_gather | solution.py:101
  677.7 0.9 fusion.132
  678.6 0.0 reduce-scatter.6.cloned.1.call-update
  678.6 74.5 %reduce-scatter.6.cloned.1.call-done = f32[16,160]{1,0:T(8,128)} async-done(((f32[128,160]{1,0:T(8,128)}), f32[16,160]{1,0:T(8,128)}) %reduce-scatter.6.cloned.1.call-update) | async-done | bytes 10256 | tf_op jit(solution)/shard_map/reduce_scatter | solution.py:102
  753.1 1.3 convert_element_type.47
  (42 shorter events, 0.2 us)
Async XLA Ops:
  6.5 671.2 %copy-start = (bf16[640,160]{0,1:T(8,128)(2,1)S(1)}, bf16[640,160]{0,1:T(8,128)(2,1)}, u32[]{:S(2)}) copy-start(bf16[640,160]{0,1:T(8,128)(2,1)} %param.11) | copy-start | bytes 614404
  6.5 66.3 %all-gather.4.cloned.1.call-start = ((), (), s32[]{:S(2)}) async-start(), calls=%async_computation.3 | async-start | bytes 1351680 | tf_op jit(solution)/shard_map/all_gather | solution.py:50
  7.3 521.1 %all-reduce.5.cloned.1.call-start = ((), (), s32[]{:S(2)}) async-start(), calls=%async_computation.5 | async-start | bytes 5242880
  97.9 16.3 %slice-start = ((s8[5242880]{0:T(1024)(128)(4,1)}), s8[1048576]{0:T(1024)(128)(4,1)S(1)}, s32[]{:S(2)}) async-start(s8[5242880]{0:T(1024)(128)(4,1)} %bitcast.101), calls=%async_computation.6 | async-start | bytes 2097152
  102.4 11.7 %slice-start.1 = ((s8[5242880]{0:T(1024)(128)(4,1)}), s8[4194304]{0:T(1024)(128)(4,1)S(1)}, s32[]{:S(2)}) async-start(s8[5242880]{0:T(1024)(128)(4,1)} %bitcast.101), calls=%async_computation.7 | async-start | bytes 8388608
  130.9 15.7 %copy-start.1 = (f32[128,5,2048]{2,0,1:T(8,128)S(1)}, f32[128,5,2048]{2,0,1:T(8,128)}, u32[]{:S(2)}) copy-start(f32[128,5,2048]{2,0,1:T(8,128)} %get-tuple-element.32) | copy-start | bytes 15728644
  130.9 15.7 %copy-start.2 = (bf16[2048,1024]{1,0:T(8,128)(2,1)S(1)}, bf16[2048,1024]{1,0:T(8,128)(2,1)}, u32[]{:S(2)}) copy-start(bf16[2048,1024]{1,0:T(8,128)(2,1)} %param.8) | copy-start | bytes 12582916
  146.6 7.5 slice-start.2
  149.0 5.0 slice-start.3
  149.0 7.6 slice-start.4
  154.1 2.5 slice-start.5
  154.1 5.0 slice-start.6
  156.6 2.5 slice-start.7
  156.6 5.0 slice-start.8
  159.1 2.5 slice-start.9
  159.1 5.0 slice-start.10
  161.6 2.5 slice-start.11
  245.5 2.2 copy-start.4
  245.5 2.8 copy-start.3
  247.7 385.6 %reduce-scatter.8.cloned.1.call-start = ((), (), s32[]{:S(2)}) async-start(), calls=%async_computation.4 | async-start | bytes 2949120
  531.6 221.6 %reduce-scatter.6.cloned.1.call-start = ((), (), s32[]{:S(2)}) async-start(), calls=%async_computation.2 | async-start | bytes 147456 | tf_op jit(solution)/shard_map/reduce_scatter | solution.py:102
Sparse Core Ops, SparseCore 0:
  9.2 63.5 all-gather.3
  247.8 280.4 all-reduce.4
  532.5 100.7 reduce-scatter.7
  678.8 74.3 reduce-scatter.5
where the time goes:
time: 763 us; the launch traced here: 761 us
  waiting for transfers between devices  347 us (45%)
  blocking collectives  292 us (38%)
  matrix products  74.5 us (10%)
  other arithmetic  19.3 us (3%)
  between operations  15.9 us (2%)
  local copies, waits for them, and re-layouts  12.6 us (2%)
    unnamed x6, waiting for transfers between devices  209 us
    unnamed x2, blocking collectives  172 us
    pmax x1, blocking collectives, per_device(): row_max = lax.pmax(block_max, ('sx', 'sy'))  76.6 us
    reduce_scatter x1, waiting for transfers between devices, per_device(): lax.psum_scatter(jnp.dot(gathered, out_weight, preferred_element_type=jnp...  74.5 us
    all_gather x1, waiting for transfers between devices, per_device(): all_queries = lax.all_gather(queries, 'sx', axis=0, tiled=True)  63.9 us
    dot_general x8, matrix products, attend_head(): lax.dot_general(query_rows, key_block, (((1,), (1,)), ((), ())), preferre...  48.7 us
    all_gather x1, blocking collectives, per_device(): gathered = lax.all_gather(attended, 'sx', axis=0, tiled=True)  43.2 us
    dot_general x8, matrix products, attend_head(): jnp.dot(rounded, value_block, preferred_element_type=jnp.float32)  24.9 us
  transfers between devices with their start and end apart: 4, of which 4 were waited for; matrix products, arithmetic and copies ran while one was open for 0% of the time, Pallas kernels for 0%

commit v1 on v0

v1 whole, which is shorter than its diff:
```python
import functools

import jax
import jax.numpy as jnp
from jax import lax
from jax.experimental import pallas as pl
from jax.experimental.pallas import tpu as pltpu
from jax.sharding import PartitionSpec as P

HQ = 40
KEY_VALUE_HEADS = 8
HEAD_SIZE = 128
GROUP = 5
LOG2E = 1.4426950408889634
BF16 = jnp.bfloat16
F32 = jnp.float32
CHIPS = 16
Y = 4
CORE_HEADS = 4
CHUNK = 1024


def attention_kernel(
    info, queries, key_own, key_pair, value_own, value_pair, scale, out, stats, bias, lhs
):
    head = pl.program_id(0)
    tokens = queries.shape[0]
    slots = key_own.shape[0]
    rows = tokens * GROUP

    @pl.when(head == 0)
    def _():
        step = 512

        def fill(i, carry):
            start = i * step
            place = lax.broadcasted_iota(jnp.int32, (step, tokens), 0) + start
            token = lax.broadcasted_iota(jnp.int32, (step, tokens), 1)
            pair = place >= slots
            entry = jnp.where(pair, place - slots, place)
            limit = jnp.where(pair, info[2], info[1])
            base = jnp.where(pair, info[4], info[3])
            seen = (entry < limit) & (base + entry <= token)
            bias[pl.ds(pl.multiple_of(start, step), step), :] = jnp.where(seen, 0.0, -1e30).astype(BF16)
            return carry

        lax.fori_loop(0, 2 * slots // step, fill, 0)

    one_hot = (
        lax.broadcasted_iota(jnp.int32, (tokens, tokens), 0)
        == lax.broadcasted_iota(jnp.int32, (tokens, tokens), 1)
    ).astype(BF16)
    for g in range(GROUP):
        lhs[g * tokens : (g + 1) * tokens, :HEAD_SIZE] = queries[:, g * HEAD_SIZE : (g + 1) * HEAD_SIZE]
        lhs[g * tokens : (g + 1) * tokens, HEAD_SIZE:] = one_hot
    left = lhs[...]
    factor = jnp.concatenate([scale[...]] * GROUP, axis=0)[:, :1]
    peak = None
    for source, (keys, values) in enumerate(((key_own, value_own), (key_pair, value_pair))):
        for start in range(0, slots, CHUNK):
            at = slice(source * slots + start, source * slots + start + CHUNK)
            right = jnp.concatenate([keys[start : start + CHUNK, :], bias[at, :]], axis=1)
            scores = lax.dot_general(
                left, right, (((1,), (1,)), ((), ())), preferred_element_type=F32
            )
            top = jnp.max(scores, axis=1, keepdims=True)
            new_peak = top if peak is None else jnp.maximum(peak, top)
            weights = jnp.exp2((scores - new_peak) * factor).astype(BF16)
            both = jnp.concatenate(
                [values[start : start + CHUNK, :], jnp.ones((CHUNK, HEAD_SIZE), BF16)], axis=1
            )
            part = jnp.dot(weights, both, preferred_element_type=F32)
            total = part if peak is None else total * jnp.exp2((peak - new_peak) * factor) + part
            peak = new_peak
    out[0] = total[:, :HEAD_SIZE].astype(BF16)
    lane = lax.broadcasted_iota(jnp.int32, (rows, HEAD_SIZE), 1)
    rest_m = jnp.broadcast_to(peak * factor, (rows, HEAD_SIZE))
    rest_l = total[:, HEAD_SIZE:]
    packed = jnp.zeros((rows, HEAD_SIZE), F32)
    for k in range(3):
        term_m = rest_m.astype(BF16).astype(F32)
        term_l = rest_l.astype(BF16).astype(F32)
        packed = jnp.where(lane == k, term_m, jnp.where(lane == 3 + k, term_l, packed))
        rest_m, rest_l = rest_m - term_m, rest_l - term_l
    stats[0] = packed.astype(BF16)


def attend(info, queries, keys, values, key_pair, value_pair, scale):
    tokens = queries.shape[0]
    slots = keys.shape[0]
    rows = tokens * GROUP
    own = pl.BlockSpec((slots, HEAD_SIZE), lambda h, s: (0, s[0] * CORE_HEADS + h))
    pair = pl.BlockSpec((slots, HEAD_SIZE), lambda h, s: (0, h))
    result = pl.BlockSpec((1, rows, HEAD_SIZE), lambda h, s: (h, 0, 0))
    return pl.pallas_call(
        attention_kernel,
        grid_spec=pltpu.PrefetchScalarGridSpec(
            num_scalar_prefetch=1,
            grid=(CORE_HEADS,),
            in_specs=[
                pl.BlockSpec((tokens, GROUP * HEAD_SIZE), lambda h, s: (0, h)),
                own,
                pair,
                own,
                pair,
                pl.BlockSpec((tokens, HEAD_SIZE), lambda h, s: (0, 0)),
            ],
            out_specs=[result, result],
            scratch_shapes=[
                pltpu.VMEM((2 * slots, tokens), BF16),
                pltpu.VMEM((rows, 2 * HEAD_SIZE), BF16),
            ],
        ),
        out_shape=[jax.ShapeDtypeStruct((CORE_HEADS, rows, HEAD_SIZE), BF16)] * 2,
        compiler_params=pltpu.CompilerParams(vmem_limit_bytes=60 * 2**20),
        cost_estimate=pl.CostEstimate(
            flops=2 * 2 * CORE_HEADS * rows * 2 * slots * 2 * HEAD_SIZE,
            bytes_accessed=2 * 2 * CORE_HEADS * 2 * slots * HEAD_SIZE,
            transcendentals=CORE_HEADS * rows * 2 * slots,
        ),
    )(info, queries, keys, key_pair, values, value_pair, scale)


def per_device(queries, keys, values, opening, valid, weight):
    sx, sy = lax.axis_index("sx"), lax.axis_index("sy")
    size_x, size_y = lax.axis_size("sx"), lax.axis_size("sy")
    core = sx % 2
    own_rows = queries.shape[0]
    tokens = own_rows * size_x
    slots = keys.shape[0]
    half = CORE_HEADS * GROUP * HEAD_SIZE
    kv_half = CORE_HEADS * HEAD_SIZE
    other_core = [(i, i ^ 1) for i in range(size_x)]

    def halves(a, width):
        mine = lax.dynamic_slice_in_dim(a, core * width, width, 1)
        return mine, lax.dynamic_slice_in_dim(a, (1 - core) * width, width, 1)

    mine, theirs = halves(queries, half)
    got = lax.ppermute(theirs, "sx", other_core)
    chip_rows = jnp.concatenate(
        [jnp.where(core == 0, mine, got), jnp.where(core == 0, got, mine)], axis=0
    )
    core_groups = [[i * 2 + c for i in range(CHIPS)] for c in range(2)]
    all_queries = lax.all_to_all(
        jnp.broadcast_to(chip_rows[None], (CHIPS, 2 * own_rows, half)),
        "sx", 0, 0, tiled=True, axis_index_groups=core_groups,
    ).reshape(tokens, half)

    key_pair = lax.ppermute(halves(keys, kv_half)[1], "sx", other_core)
    value_pair = lax.ppermute(halves(values, kv_half)[1], "sx", other_core)
    valid_pair = lax.ppermute(valid, "sx", other_core)

    far = lax.ppermute(weight, "sy", [(i, i ^ Y) for i in range(size_y)])
    near = jnp.stack([weight, far])
    blocks = [near] + [lax.ppermute(near, "sy", [(i, i ^ k) for i in range(size_y)]) for k in (1, 2, 3)]

    base = (sx * size_y + sy) * slots - opening[0]
    base_pair = ((sx ^ 1) * size_y + sy) * slots - opening[0]
    info = jnp.stack([core, valid[0], valid_pair[0], base, base_pair]).astype(jnp.int32)
    positions = opening[0] + jnp.arange(tokens, dtype=jnp.int32)
    buckets = ((positions + 1) // 8192).astype(F32)
    temper = (1.0 + 0.1 * jnp.log(buckets + 1.0)) * HEAD_SIZE ** (-0.5)
    scale = jnp.broadcast_to((temper * LOG2E)[:, None], (tokens, HEAD_SIZE))
    out, stats = attend(info, all_queries, keys, values, key_pair, value_pair, scale)

    z_lo = CHIPS // CORE_HEADS
    sub = tokens // size_y // z_lo
    piece_rows = GROUP * sub
    pieces = out.reshape(CORE_HEADS, GROUP, size_y, z_lo, sub, HEAD_SIZE).transpose(0, 3, 2, 1, 4, 5)
    pieces = pieces.reshape(CHIPS * size_y, piece_rows, HEAD_SIZE)
    extra = stats[..., :6].reshape(CORE_HEADS, GROUP, size_y, z_lo, sub, 6).transpose(0, 3, 2, 5, 1, 4)
    extra = extra.reshape(CHIPS * size_y, 1, 6 * piece_rows)
    extra = jnp.pad(extra, ((0, 0), (0, 0), (0, HEAD_SIZE - 6 * piece_rows)))
    all_groups = [
        [(i * 2 + c) * size_y + j for i in range(CHIPS) for j in range(size_y)] for c in range(2)
    ]
    received = lax.all_to_all(
        jnp.concatenate([pieces, extra], axis=1),
        ("sx", "sy"), 0, 0, tiled=True, axis_index_groups=all_groups,
    )
    terms = received[:, piece_rows, : 6 * piece_rows].astype(F32).reshape(-1, 2, 3, piece_rows)
    terms = terms[:, :, 0] + (terms[:, :, 1] + terms[:, :, 2])
    peak, total = terms[:, 0], terms[:, 1]
    share = jnp.exp2(peak - jnp.max(peak, axis=0))
    summed = jnp.sum(received[:, :piece_rows].astype(F32) * share[..., None], axis=0)
    attended = (summed / jnp.sum(share * total, axis=0)[:, None]).astype(BF16)

    gathered = lax.all_to_all(
        jnp.broadcast_to(attended[None], (size_x, piece_rows, HEAD_SIZE)), "sx", 0, 0, tiled=True
    )
    gathered = gathered.reshape(CORE_HEADS, z_lo, 2, GROUP, sub, HEAD_SIZE).transpose(2, 0, 1, 4, 3, 5)
    gathered = gathered.reshape(KEY_VALUE_HEADS, z_lo * sub, GROUP * HEAD_SIZE)
    result = jnp.zeros((z_lo * sub, weight.shape[1]), F32)
    for k, block in enumerate(blocks):
        for f in range(2):
            rows = lax.dynamic_index_in_dim(gathered, (sy ^ k) ^ (Y * f), 0, keepdims=False)
            result = result + jnp.dot(rows, block[f], preferred_element_type=F32)
    return result.astype(BF16)


def solution(mesh):
    return jax.shard_map(
        per_device,
        mesh=mesh,
        in_specs=(
            P("sx", None),
            P(("sx", "sy"), None),
            P(("sx", "sy"), None),
            P(),
            P(("sx", "sy")),
            P("sy", "sx"),
        ),
        out_specs=P("sy", "sx"),
        check_vma=False,
    )
```

time: 763 us -> 134 us (0.18)
  waiting for transfers between devices: 347 us -> 50.5 us
  blocking collectives: 292 us -> 0 us
  matrix products: 74.5 us -> 2.04 us
  starting transfers between devices: 0.12 us -> 42.1 us
  Pallas kernels: 0 us -> 20 us
  other arithmetic: 19.3 us -> 1.03 us
  between operations: 15.9 us -> 1.55 us
    unnamed x6 -> x0, waiting for transfers between devices: 209 us -> none
    unnamed x2 -> x0, blocking collectives: 172 us -> none
    pmax x1 -> x0, blocking collectives: 76.6 us -> none  [per_device(): row_max = lax.pmax(block_max, ('sx', 'sy'))]
    reduce_scatter x1 -> x0, waiting for transfers between devices: 74.5 us -> none  [per_device(): lax.psum_scatter(jnp.dot(gathered, out_weight, preferred_element_type=jnp...]
    dot_general x17 -> x8, matrix products: 74.5 us -> 2.04 us  [per_device(): result = result + jnp.dot(rows, block[f], preferred_element_type=F32)]
    all_gather x1 -> x0, waiting for transfers between devices: 63.9 us -> none  [per_device(): all_queries = lax.all_gather(queries, 'sx', axis=0, tiled=True)]
    all_gather x1 -> x0, blocking collectives: 43.2 us -> none  [per_device(): gathered = lax.all_gather(attended, 'sx', axis=0, tiled=True)]
    all_to_all x0 -> x3, waiting for transfers between devices: none -> 39.4 us  [the longest x1 17.4 us: per_device(): lax.all_to_all(jnp.concatenate([pieces, extra], axis=1), ('sx', 'sy'), 0,...]
  transfers between devices with their start and end apart: 4 -> 11, of which waited for: 4 -> 5; matrix products, arithmetic and copies ran while one was open for 0% -> 6% of each run, Pallas kernels for 0% -> 0%
where the time goes in v1:
time: 134 us; the launch traced here: 133 us
  waiting for transfers between devices  50.5 us (38%)
  starting transfers between devices  42.1 us (31%)
  Pallas kernels  20 us (15%)
  local copies, waits for them, and re-layouts  16.1 us (12%)
  matrix products  2.04 us (2%)
  between operations  1.55 us (1%)
    pallas_call x1, Pallas kernels, attend(): pl.pallas_call(attention_kernel, grid_spec=pltpu.PrefetchScalarGridSpec(n...  20 us
    all_to_all x1, waiting for transfers between devices, per_device(): lax.all_to_all(jnp.concatenate([pieces, extra], axis=1), ('sx', 'sy'), 0,...  17.4 us
    all_to_all x1, waiting for transfers between devices, per_device(): lax.all_to_all(jnp.broadcast_to(chip_rows[None], (CHIPS, 2 * own_rows, ha...  15.5 us
    all_to_all x1, starting transfers between devices, per_device(): lax.all_to_all(jnp.broadcast_to(attended[None], (size_x, piece_rows, HEAD...  12.5 us
    ppermute x3, waiting for transfers between devices, per_device(): lax.ppermute(near, 'sy', [(i, i ^ k) for i in range(size_y)])  11.1 us
    all_to_all x1, starting transfers between devices, per_device(): lax.all_to_all(jnp.concatenate([pieces, extra], axis=1), ('sx', 'sy'), 0,...  10.6 us
    all_to_all x1, waiting for transfers between devices, per_device(): lax.all_to_all(jnp.broadcast_to(attended[None], (size_x, piece_rows, HEAD...  6.49 us
    all_to_all x1, starting transfers between devices, per_device(): lax.all_to_all(jnp.broadcast_to(chip_rows[None], (CHIPS, 2 * own_rows, ha...  6.45 us
  transfers between devices with their start and end apart: 11, of which 5 were waited for; matrix products, arithmetic and copies ran while one was open for 6% of the time, Pallas kernels for 0%

profile of v1, /device:TPU:1, one launch (start us, length us, event | category | flops | bytes accessed | tf_op | source)
XLA Modules:
  0.0 133.4 jit_solution(16609692766184840537)
XLA Ops:
  0.0 0.0 copy-start.2
  0.0 1.7 %constant_dynamic-slice_fusion.1 = bf16[2048,512]{1,0:T(8,128)(2,1)S(1)} fusion(bf16[2048,1024]{1,0:T(8,128)(2,1)} %key_own.1, s32[]{:T(128)S(6)} %select_n.69), kind=kLoop, calls=%fused_computation.64 | loop fusion | bytes 4194308 | tf_op jit(solution)/shard_map/dynamic_slice | solution.py:137
  1.7 3.3 %collective-permute-start.2 = (bf16[2048,512]{1,0:T(8,128)(2,1)S(1)}, bf16[2048,512]{1,0:T(8,128)(2,1)}, u32[]{:S(2)}, u32[]{:S(2)}) collective-permute-start(bf16[2048,512]{1,0:T(8,128)(2,1)S(1)} %constant_dynamic-slice_fusion.1), channel_id=1, source_target_pairs={{0,8},{8,0},{16,24},{24,16},{32,40},{40,32},{48,56},{56,48},{64,72... | collective-permute-start | bytes 6291464 | tf_op jit(solution)/shard_map/ppermute | solution.py:150
  5.1 0.0 copy-done.2
  5.1 0.1 collective-permute-start.1
  5.2 3.0 %constant_dynamic-slice_fusion = bf16[2048,512]{1,0:T(8,128)(2,1)} fusion(bf16[2048,1024]{1,0:T(8,128)(2,1)} %value_own.1, s32[]{:T(128)S(6)} %select_n.69), kind=kLoop, calls=%fused_computation.63 | loop fusion | bytes 4194308 | tf_op jit(solution)/shard_map/dynamic_slice | solution.py:137
  8.3 0.5 collective-permute-start.3
  8.7 0.0 collective-permute-done.1
  8.8 0.9 broadcast_in_dim.6
  9.7 6.4 %all-to-all-start = ((bf16[16,8,2560]{2,1,0:T(8,128)(2,1)}), bf16[16,8,2560]{2,1,0:T(8,128)(2,1)S(1)}, u32[]{:S(2)}, u32[]{:S(2)}) async-start(bf16[16,8,2560]{2,1,0:T(8,128)(2,1)} %broadcast_in_dim.6), calls=%async_computation | async-start | bytes 1310720 | tf_op jit(solution)/shard_map/all_to_all | solution.py:145
  16.1 0.5 collective-permute-start
  18.0 0.0 collective-permute-done
  18.0 1.4 %stack.24.info = s32[5]{0:T(128)} concatenate(s32[1]{0:T(128)} %bitcast, s32[1]{0:T(128)S(6)} %copy.31, s32[1]{0:T(128)} %collective-permute-done, s32[1]{0:T(128)} %bitcast.2, s32[1]{0:T(128)} %bitcast.3), dimensions={0} | concatenate | bytes 40 | tf_op jit(solution)/shard_map/stack | solution.py:160
  19.4 15.5 %all-to-all-done = bf16[16,8,2560]{2,1,0:T(8,128)(2,1)S(1)} async-done(((bf16[16,8,2560]{2,1,0:T(8,128)(2,1)}), bf16[16,8,2560]{2,1,0:T(8,128)(2,1)S(1)}, u32[]{:S(2)}, u32[]{:S(2)}) %all-to-all-start) | async-done | bytes 655392 | tf_op jit(solution)/shard_map/all_to_all | solution.py:145
  34.8 0.0 copy-start.1
  34.8 0.0 collective-permute-done.2.key_pair
  34.9 0.0 collective-permute-done.3.value_pair
  34.9 0.8 broadcast_in_dim.7.scale
  35.7 0.0 copy-done.1
  35.7 20.0 %shard_map.64 = (bf16[4,640,128]{2,1,0:T(8,128)(2,1)}, bf16[4,640,128]{2,1,0:T(8,128)(2,1)}) custom-call(s32[5]{0:T(128)} %stack.24.info, bf16[128,2560]{1,0:T(8,128)(2,1)} %bitcast.87, bf16[2048,1024]{1,0:T(8,128)(2,1)} %key_own.1, bf16[2048,512]{1,0:T(8,128)(2,1)} %collective-permute-done.2.key_pair, bf16[2048,1024]{1,0:T(8,128)(2,1)} %value_own.1, ...), custom_call_target="tpu_custom_call" | custom-call | flops 10737418240 | bytes 8388608 | tf_op jit(solution)/shard_map/pallas_call | solution.py:95
  55.7 1.3 copy.21
  57.0 3.7 %copy.22 = bf16[4,5,8,4,4,6]{2,3,0,4,1,5:T(4,128)(2,1)S(1)} copy(bf16[4,5,8,4,4,6]{5,4,3,2,1,0:T(4,128)(2,1)} %bitcast.88) | data formatting | bytes 61440 | tf_op jit(solution)/shard_map/reshape | solution.py:172
  60.6 0.5 reshape.91
  61.1 0.1 copy.23
  61.2 0.0 copy-start
  61.2 0.1 fusion.7
  61.3 1.4 %copy.24 = bf16[128,21,128]{2,1,0:T(8,128)(2,1)} copy(bf16[128,21,128]{2,0,1:T(8,128)(2,1)S(1)} %fusion.7) | data formatting | bytes 1376256 | tf_op jit(solution)/shard_map/concatenate | solution.py:179
  62.6 10.6 %all-to-all-start.1 = ((bf16[128,21,128]{2,1,0:T(8,128)(2,1)}), bf16[128,21,128]{2,1,0:T(8,128)(2,1)S(1)}, u32[]{:S(2)}, u32[]{:S(2)}) async-start(bf16[128,21,128]{2,1,0:T(8,128)(2,1)} %copy.24), calls=%async_computation.1 | async-start | bytes 1572864 | tf_op jit(solution)/shard_map/all_to_all | solution.py:178
  73.3 0.0 copy-done
  73.3 4.7 %collective-permute-start.4 = (bf16[640,160]{0,1:T(8,128)(2,1)S(1)}, bf16[640,160]{0,1:T(8,128)(2,1)S(1)}, u32[]{:S(2)}, u32[]{:S(2)}) collective-permute-start(bf16[640,160]{0,1:T(8,128)(2,1)S(1)} %copy-done), channel_id=1, source_target_pairs={{0,4},{1,5},{2,6},{3,7},{4,0},{5,1},{6,2},{7,3},{8,12},{9,13},{10,... | collective-permute-start | bytes 614408 | tf_op jit(solution)/shard_map/ppermute | solution.py:154
  78.1 17.4 %all-to-all-done.1 = bf16[128,21,128]{2,1,0:T(8,128)(2,1)S(1)} async-done(((bf16[128,21,128]{2,1,0:T(8,128)(2,1)}), bf16[128,21,128]{2,1,0:T(8,128)(2,1)S(1)}, u32[]{:S(2)}, u32[]{:S(2)}) %all-to-all-start.1) | async-done | bytes 688160 | tf_op jit(solution)/shard_map/all_to_all | solution.py:178
  95.5 0.1 slice.57
  95.6 0.1 copy.29
  95.7 0.1 slice_reduce_fusion
  95.8 0.2 fusion.33
  96.0 0.1 copy.26
  96.1 0.5 multiply_reduce_fusion
  96.6 0.1 divide_convert_fusion
  96.7 0.7 broadcast_in_dim.8
  97.4 12.5 %all-to-all-start.2 = ((bf16[32,20,128]{2,1,0:T(8,128)(2,1)}), bf16[32,20,128]{2,1,0:T(8,128)(2,1)S(1)}, u32[]{:S(2)}, u32[]{:S(2)}) async-start(bf16[32,20,128]{2,1,0:T(8,128)(2,1)} %broadcast_in_dim.8), calls=%async_computation.2 | async-start | bytes 393216 | tf_op jit(solution)/shard_map/all_to_all | solution.py:189
  109.9 0.0 collective-permute-done.4
  110.0 0.1 collective-permute-start.6
  110.1 2.0 %collective-permute-start.5 = (bf16[2,640,160]{1,2,0:T(8,128)(2,1)S(1)}, bf16[2,640,160]{1,2,0:T(8,128)(2,1)S(1)}, u32[]{:S(2)}, u32[]{:S(2)}) collective-permute-start(bf16[2,640,160]{1,2,0:T(8,128)(2,1)S(1)} %pad_maximum_fusion), channel_id=1, source_target_pairs={{0,1},{1,0},{2,3},{3,2},{4,5},{5,4},{6,7},{7,6},{8,9},{9,8},{10,11... | collective-permute-start | bytes 1228808 | tf_op jit(solution)/shard_map/ppermute | solution.py:156
  112.1 1.2 collective-permute-start.7
  113.3 6.5 %all-to-all-done.2 = bf16[32,20,128]{2,1,0:T(8,128)(2,1)S(1)} async-done(((bf16[32,20,128]{2,1,0:T(8,128)(2,1)}), bf16[32,20,128]{2,1,0:T(8,128)(2,1)S(1)}, u32[]{:S(2)}, u32[]{:S(2)}) %all-to-all-start.2) | async-done | bytes 163872 | tf_op jit(solution)/shard_map/all_to_all | solution.py:189
  119.8 0.1 copy.28
  120.0 0.2 reshape.93
  120.2 0.1 fusion.22
  120.3 2.1 %collective-permute-done.6 = bf16[2,640,160]{1,2,0:T(8,128)(2,1)S(1)} collective-permute-done((bf16[2,640,160]{1,2,0:T(8,128)(2,1)S(1)}, bf16[2,640,160]{1,2,0:T(8,128)(2,1)S(1)}, u32[]{:S(2)}, u32[]{:S(2)}) %collective-permute-start.6) | collective-permute-done | bytes 409632 | tf_op jit(solution)/shard_map/ppermute | solution.py:156
  122.4 0.1 fusion.11
  122.6 0.2 fusion.10
  122.8 9.0 %collective-permute-done.7 = bf16[2,640,160]{1,2,0:T(8,128)(2,1)S(1)} collective-permute-done((bf16[2,640,160]{1,2,0:T(8,128)(2,1)S(1)}, bf16[2,640,160]{1,2,0:T(8,128)(2,1)S(1)}, u32[]{:S(2)}, u32[]{:S(2)}) %collective-permute-start.7) | collective-permute-done | bytes 409632 | tf_op jit(solution)/shard_map/ppermute | solution.py:156
  131.7 0.1 fusion.9
  131.9 0.2 fusion.8
  132.1 0.2 convolution_add_fusion.1
  132.3 0.0 collective-permute-done.5
  132.3 0.2 fusion.12
  132.5 0.9 fusion.6
  (8 shorter events, 0.2 us)
Async XLA Ops:
  0.0 5.1 %copy-start.2 = (bf16[4,5120]{1,0:T(4,128)(2,1)S(1)}, bf16[4,5120]{1,0:T(4,128)(2,1)}, u32[]{:S(2)}) copy-start(bf16[4,5120]{1,0:T(4,128)(2,1)} %param.6) | copy-start | bytes 122884
  1.7 33.1 %collective-permute-start.2 = (bf16[2048,512]{1,0:T(8,128)(2,1)S(1)}, bf16[2048,512]{1,0:T(8,128)(2,1)}, u32[]{:S(2)}, u32[]{:S(2)}) collective-permute-start(bf16[2048,512]{1,0:T(8,128)(2,1)S(1)} %constant_dynamic-slice_fusion.1), channel_id=1, source_target_pairs={{0,8},{8,0},{16,24},{24,16},{32,40},{40,32},{48,56},{56,48},{64,72... | collective-permute-start | bytes 6291464 | tf_op jit(solution)/shard_map/ppermute | solution.py:150
  5.1 3.7 %collective-permute-start.1 = (bf16[4,2560]{1,0:T(4,128)(2,1)S(1)}, bf16[4,2560]{1,0:T(4,128)(2,1)S(1)}, u32[]{:S(2)}, u32[]{:S(2)}) collective-permute-start(bf16[4,2560]{1,0:T(4,128)(2,1)S(1)} %constant_dynamic-slice_fusion.2), channel_id=1, source_target_pairs={{0,8},{8,0},{16,24},{24,16},{32,40},{40,32},{48,56},{56,48},{64,72... | collective-permute-start | bytes 61448 | tf_op jit(solution)/shard_map/ppermute | solution.py:140
  8.3 26.6 %collective-permute-start.3 = (bf16[2048,512]{1,0:T(8,128)(2,1)}, bf16[2048,512]{1,0:T(8,128)(2,1)}, u32[]{:S(2)}, u32[]{:S(2)}) collective-permute-start(bf16[2048,512]{1,0:T(8,128)(2,1)} %constant_dynamic-slice_fusion), channel_id=1, source_target_pairs={{0,8},{8,0},{16,24},{24,16},{32,40},{40,32},{48,56},{56,48},{64,72... | collective-permute-start | bytes 6291464 | tf_op jit(solution)/shard_map/ppermute | solution.py:151
  9.7 25.2 %all-to-all-start = ((bf16[16,8,2560]{2,1,0:T(8,128)(2,1)}), bf16[16,8,2560]{2,1,0:T(8,128)(2,1)S(1)}, u32[]{:S(2)}, u32[]{:S(2)}) async-start(bf16[16,8,2560]{2,1,0:T(8,128)(2,1)} %broadcast_in_dim.6), calls=%async_computation | async-start | bytes 1310720 | tf_op jit(solution)/shard_map/all_to_all | solution.py:145
  16.1 1.9 %collective-permute-start = (s32[1]{0:T(128)}, s32[1]{0:T(128)}, u32[]{:S(2)}, u32[]{:S(2)}) collective-permute-start(s32[1]{0:T(128)} %param.10), channel_id=1, source_target_pairs={{0,8},{8,0},{16,24},{24,16},{32,40},{40,32},{48,56},{56,48},{64,72... | collective-permute-start | bytes 20 | tf_op jit(solution)/shard_map/ppermute | solution.py:152
  34.8 0.9 copy-start.1
  61.2 12.1 %copy-start = (bf16[640,160]{0,1:T(8,128)(2,1)S(1)}, bf16[640,160]{0,1:T(8,128)(2,1)}, u32[]{:S(2)}) copy-start(bf16[640,160]{0,1:T(8,128)(2,1)} %param.11) | copy-start | bytes 614404
  62.6 32.8 %all-to-all-start.1 = ((bf16[128,21,128]{2,1,0:T(8,128)(2,1)}), bf16[128,21,128]{2,1,0:T(8,128)(2,1)S(1)}, u32[]{:S(2)}, u32[]{:S(2)}) async-start(bf16[128,21,128]{2,1,0:T(8,128)(2,1)} %copy.24), calls=%async_computation.1 | async-start | bytes 1572864 | tf_op jit(solution)/shard_map/all_to_all | solution.py:178
  73.3 36.6 %collective-permute-start.4 = (bf16[640,160]{0,1:T(8,128)(2,1)S(1)}, bf16[640,160]{0,1:T(8,128)(2,1)S(1)}, u32[]{:S(2)}, u32[]{:S(2)}) collective-permute-start(bf16[640,160]{0,1:T(8,128)(2,1)S(1)} %copy-done), channel_id=1, source_target_pairs={{0,4},{1,5},{2,6},{3,7},{4,0},{5,1},{6,2},{7,3},{8,12},{9,13},{10,... | collective-permute-start | bytes 614408 | tf_op jit(solution)/shard_map/ppermute | solution.py:154
  97.4 22.4 %all-to-all-start.2 = ((bf16[32,20,128]{2,1,0:T(8,128)(2,1)}), bf16[32,20,128]{2,1,0:T(8,128)(2,1)S(1)}, u32[]{:S(2)}, u32[]{:S(2)}) async-start(bf16[32,20,128]{2,1,0:T(8,128)(2,1)} %broadcast_in_dim.8), calls=%async_computation.2 | async-start | bytes 393216 | tf_op jit(solution)/shard_map/all_to_all | solution.py:189
  110.0 12.5 %collective-permute-start.6 = (bf16[2,640,160]{1,2,0:T(8,128)(2,1)S(1)}, bf16[2,640,160]{1,2,0:T(8,128)(2,1)S(1)}, u32[]{:S(2)}, u32[]{:S(2)}) collective-permute-start(bf16[2,640,160]{1,2,0:T(8,128)(2,1)S(1)} %pad_maximum_fusion), channel_id=1, source_target_pairs={{0,2},{1,3},{2,0},{3,1},{4,6},{5,7},{6,4},{7,5},{8,10},{9,11},{10,... | collective-permute-start | bytes 1228808 | tf_op jit(solution)/shard_map/ppermute | solution.py:156
  110.1 22.2 %collective-permute-start.5 = (bf16[2,640,160]{1,2,0:T(8,128)(2,1)S(1)}, bf16[2,640,160]{1,2,0:T(8,128)(2,1)S(1)}, u32[]{:S(2)}, u32[]{:S(2)}) collective-permute-start(bf16[2,640,160]{1,2,0:T(8,128)(2,1)S(1)} %pad_maximum_fusion), channel_id=1, source_target_pairs={{0,1},{1,0},{2,3},{3,2},{4,5},{5,4},{6,7},{7,6},{8,9},{9,8},{10,11... | collective-permute-start | bytes 1228808 | tf_op jit(solution)/shard_map/ppermute | solution.py:156
  112.1 19.6 %collective-permute-start.7 = (bf16[2,640,160]{1,2,0:T(8,128)(2,1)S(1)}, bf16[2,640,160]{1,2,0:T(8,128)(2,1)S(1)}, u32[]{:S(2)}, u32[]{:S(2)}) collective-permute-start(bf16[2,640,160]{1,2,0:T(8,128)(2,1)S(1)} %pad_maximum_fusion), channel_id=1, source_target_pairs={{0,3},{1,2},{2,1},{3,0},{4,7},{5,6},{6,5},{7,4},{8,11},{9,10},{10,... | collective-permute-start | bytes 1228808 | tf_op jit(solution)/shard_map/ppermute | solution.py:156

commit v2 on v1

v2 whole, which is shorter than its diff:
```python
import jax
import jax.numpy as jnp
from jax import lax
from jax.experimental import pallas as pl
from jax.experimental.pallas import tpu as pltpu
from jax.sharding import PartitionSpec as P

HQ = 40
KEY_VALUE_HEADS = 8
HEAD_SIZE = 128
GROUP = 5
LOG2E = 1.4426950408889634
BF16 = jnp.bfloat16
F32 = jnp.float32
CHIPS = 16
Y = 4
CORE_HEADS = 4
CHUNK = 1024
TILE = 16
PIECE = 2 * GROUP * TILE
STATS = 16
SMALL = 24


def attention_kernel(
    info, valid_pair, q0, q1, q2, q3, key_own, key_pair, value_own, value_pair, out, bias, lhs, factors
):
    head = pl.program_id(0)
    rows = lhs.shape[0]
    tokens = rows // GROUP
    slots = key_own.shape[0]
    tiles = tokens // TILE

    @pl.when(head == 0)
    def _():
        step = 512

        def fill(i, carry):
            start = i * step
            place = lax.broadcasted_iota(jnp.int32, (step, tokens), 0) + start
            token = lax.broadcasted_iota(jnp.int32, (step, tokens), 1)
            pair = place >= slots
            entry = jnp.where(pair, place - slots, place)
            limit = jnp.where(pair, valid_pair[0], info[1])
            base = jnp.where(pair, info[3], info[2])
            seen = (entry < limit) & (base + entry <= token)
            bias[pl.ds(pl.multiple_of(start, step), step), :] = jnp.where(seen, 0.0, -1e30).astype(BF16)
            return carry

        lax.fori_loop(0, 2 * slots // step, fill, 0)
        token = lax.broadcasted_iota(jnp.int32, (tokens, HEAD_SIZE), 0)
        buckets = ((info[4] + token + 1) >> 13).astype(F32)
        scale = (1.0 + 0.1 * jnp.log(buckets + 1.0)) * (HEAD_SIZE ** (-0.5) * LOG2E)
        row = lax.broadcasted_iota(jnp.int32, (TILE, tokens), 0)
        lane = lax.broadcasted_iota(jnp.int32, (TILE, tokens), 1)
        for slot in range(tiles):
            first = ((slot % 2) * Y + slot // 2) * TILE
            one_hot = (lane == row + first).astype(BF16)
            for g in range(GROUP):
                at = slice((slot * GROUP + g) * TILE, (slot * GROUP + g + 1) * TILE)
                lhs[at, HEAD_SIZE:] = one_hot
                factors[at, :] = scale[first : first + TILE]

    for k, block in enumerate((q0, q1, q2, q3)):
        x = info[5 + k]
        for b in range(2):
            slot = ((x % 2) * 2 + b) * 2 + x // 2
            for g in range(GROUP):
                at = pl.multiple_of((slot * GROUP + g) * TILE, TILE)
                lhs[pl.ds(at, TILE), :HEAD_SIZE] = block[
                    b * TILE : (b + 1) * TILE, g * HEAD_SIZE : (g + 1) * HEAD_SIZE
                ]
    left = lhs[...]
    factor = factors[:, :1]
    peak = None
    for source, (keys, values) in enumerate(((key_own, value_own), (key_pair, value_pair))):
        for start in range(0, slots, CHUNK):
            at = slice(source * slots + start, source * slots + start + CHUNK)
            right = jnp.concatenate([keys[start : start + CHUNK, :], bias[at, :]], axis=1)
            scores = lax.dot_general(
                left, right, (((1,), (1,)), ((), ())), preferred_element_type=F32
            )
            top = jnp.max(scores, axis=1, keepdims=True)
            new_peak = top if peak is None else jnp.maximum(peak, top)
            weights = jnp.exp2((scores - new_peak) * factor).astype(BF16)
            both = jnp.concatenate(
                [values[start : start + CHUNK, :], jnp.ones((CHUNK, HEAD_SIZE), BF16)], axis=1
            )
            part = jnp.dot(weights, both, preferred_element_type=F32)
            total = part if peak is None else total * jnp.exp2((peak - new_peak) * factor) + part
            peak = new_peak
    lane = lax.broadcasted_iota(jnp.int32, (rows, HEAD_SIZE), 1)
    rest_m = jnp.broadcast_to(peak * factor, (rows, HEAD_SIZE))
    rest_l = total[:, HEAD_SIZE:]
    packed = jnp.zeros((rows, HEAD_SIZE), F32)
    for k in range(3):
        term_m = rest_m.astype(BF16).astype(F32)
        term_l = rest_l.astype(BF16).astype(F32)
        packed = jnp.where(lane == k, term_m, jnp.where(lane == 3 + k, term_l, packed))
        rest_m, rest_l = rest_m - term_m, rest_l - term_l
    packed = packed.astype(BF16)
    pick = (
        lax.broadcasted_iota(jnp.int32, (8, HEAD_SIZE), 0)
        == lax.broadcasted_iota(jnp.int32, (8, HEAD_SIZE), 1)
    ).astype(BF16)
    for y in range(Y):
        at = slice(y * PIECE, (y + 1) * PIECE)
        out[0, y, :PIECE, :] = total[at, :HEAD_SIZE].astype(BF16)
        turned = lax.dot_general(
            pick, packed[at, :], (((1,), (1,)), ((), ())), preferred_element_type=F32
        )
        second = jnp.concatenate(
            [turned[:, HEAD_SIZE:], jnp.zeros((8, 2 * HEAD_SIZE - PIECE), F32)], axis=1
        )
        out[0, y, PIECE:, :] = jnp.concatenate([turned[:, :HEAD_SIZE], second], axis=0).astype(BF16)


def attend(info, valid_pair, queries, keys, values, key_pair, value_pair):
    tokens = queries[0].shape[0] * 4
    slots = keys.shape[0]
    rows = tokens * GROUP
    cache = pl.BlockSpec((slots, HEAD_SIZE), lambda h, s, v: (0, s[0] * CORE_HEADS + h))
    quarter = pl.BlockSpec((tokens // 4, GROUP * HEAD_SIZE), lambda h, s, v: (0, h))
    return pl.pallas_call(
        attention_kernel,
        grid_spec=pltpu.PrefetchScalarGridSpec(
            num_scalar_prefetch=2,
            grid=(CORE_HEADS,),
            in_specs=[
                quarter,
                quarter,
                quarter,
                quarter,
                cache,
                cache,
                cache,
                cache,
            ],
            out_specs=pl.BlockSpec((1, Y, PIECE + STATS, HEAD_SIZE), lambda h, s, v: (h, 0, 0, 0)),
            scratch_shapes=[
                pltpu.VMEM((2 * slots, tokens), BF16),
                pltpu.VMEM((rows, 2 * HEAD_SIZE), BF16),
                pltpu.VMEM((rows, HEAD_SIZE), F32),
            ],
        ),
        out_shape=jax.ShapeDtypeStruct((CORE_HEADS, Y, PIECE + STATS, HEAD_SIZE), BF16),
        compiler_params=pltpu.CompilerParams(vmem_limit_bytes=60 * 2**20),
        cost_estimate=pl.CostEstimate(
            flops=2 * 2 * CORE_HEADS * rows * 2 * slots * 2 * HEAD_SIZE,
            bytes_accessed=2 * 2 * CORE_HEADS * 2 * slots * HEAD_SIZE,
            transcendentals=CORE_HEADS * rows * 2 * slots,
        ),
    )(info, valid_pair, *queries, keys, key_pair, values, value_pair)


def merge(out, peak, total):
    top = jnp.max(peak, axis=0)
    share = jnp.exp2(peak - top)
    return jnp.sum(out * share[..., None], axis=0), top, jnp.sum(share * total, axis=0)


def per_device(queries, keys, values, opening, valid, weight):
    sx, sy = lax.axis_index("sx"), lax.axis_index("sy")
    size_x, size_y = lax.axis_size("sx"), lax.axis_size("sy")
    core, z_lo, x = sx % 2, (sx // 2) % 4, sx // 8
    own_rows = queries.shape[0]
    tokens = own_rows * size_x
    slots = keys.shape[0]
    half = CORE_HEADS * GROUP * HEAD_SIZE

    def swap(a, axis, bits):
        size = lax.axis_size(axis)
        return lax.ppermute(a, axis, [(i, i ^ bits) for i in range(size)])

    got = swap(queries, "sx", 1)
    chip_rows = jnp.concatenate(
        [jnp.where(core == 0, queries, got), jnp.where(core == 0, got, queries)], axis=0
    )
    chip_rows = lax.dynamic_slice_in_dim(chip_rows, core * half, half, 1)
    chip_rows, keys, values, valid = lax.optimization_barrier((chip_rows, keys, values, valid))
    line = jnp.stack([chip_rows] + [swap(chip_rows, "sx", 2 * k) for k in (1, 2, 3)])
    line = jnp.concatenate(
        [lax.dynamic_index_in_dim(line, z_lo ^ k, 0, keepdims=False) for k in range(4)], axis=0
    )
    line, weight = lax.optimization_barrier((line, weight.T))
    far = swap(weight, "sy", Y)
    all_queries = [line] + [swap(line, "sx", 8 * k) for k in (1, 2, 3)]

    valid_pair = swap(valid, "sx", 1)
    key_pair = swap(keys, "sx", 1)
    value_pair = swap(values, "sx", 1)

    base = (sx * size_y + sy) * slots - opening[0]
    base_pair = ((sx ^ 1) * size_y + sy) * slots - opening[0]
    info = jnp.stack(
        [core, valid[0], base, base_pair, opening[0]] + [x ^ k for k in range(4)]
    ).astype(jnp.int32)
    out = attend(info, valid_pair, all_queries, keys, values, key_pair, value_pair)

    def device(x, z_lo, core, z_hi, y):
        return ((x * 4 + z_lo) * 2 + core) * size_y + z_hi * Y + y

    four, two = range(4), range(2)
    planes = [
        [device(x, z, c, h, y) for x in four for y in four] for z in four for c in two for h in two
    ]
    received = lax.all_to_all(
        out.reshape(CHIPS, PIECE + STATS, HEAD_SIZE),
        ("sx", "sy"), 0, 0, tiled=True, axis_index_groups=planes,
    )
    received, far = lax.optimization_barrier((received, far))
    near = jnp.stack([weight, far])
    near_1, near_3 = swap(near, "sy", 1), swap(near, "sy", 3)
    terms = received[:, PIECE:].astype(F32).reshape(CHIPS, 2, 8, HEAD_SIZE)
    peak = (terms[:, :, 0] + (terms[:, :, 1] + terms[:, :, 2])).reshape(CHIPS, -1)[:, :PIECE]
    total = (terms[:, :, 3] + (terms[:, :, 4] + terms[:, :, 5])).reshape(CHIPS, -1)[:, :PIECE]
    out, peak, total = merge(received[:, :PIECE].astype(F32), peak, total)

    def small(a, fill):
        a = a.reshape((2, PIECE // 2) + a.shape[1:])
        pad = [(0, 0), (0, 4 * SMALL - PIECE // 2)] + [(0, 0)] * (a.ndim - 2)
        a = jnp.pad(a, pad, constant_values=fill)
        return a.reshape((size_y, SMALL) + a.shape[2:])

    stats = jnp.stack([small(peak, 0.0), small(total, 1.0)], axis=1)
    stats = jnp.pad(stats, ((0, 0), (0, 6), (0, HEAD_SIZE - SMALL)))
    lines = [
        [device(x, z, c, h, y) for h in two for z in four] for x in four for c in two for y in four
    ]
    received = lax.all_to_all(
        jnp.concatenate([small(out, 0.0), stats], axis=1),
        ("sx", "sy"), 0, 0, tiled=True, axis_index_groups=lines,
    )
    received, near_1, near_3 = lax.optimization_barrier((received, near_1, near_3))
    blocks = [near, near_1, swap(near_3, "sy", 1), near_3]
    out, _, total = merge(received[:, :SMALL], received[:, SMALL, :SMALL], received[:, SMALL + 1, :SMALL])
    attended = (out / total[:, None]).astype(BF16)

    gathered = lax.all_to_all(
        jnp.broadcast_to(attended[None], (size_x, SMALL, HEAD_SIZE)), "sx", 0, 0, tiled=True
    )
    gathered = gathered.reshape(4, 4, 2, SMALL, HEAD_SIZE).transpose(2, 0, 1, 3, 4)
    gathered = gathered.reshape(KEY_VALUE_HEADS, 4 * SMALL, HEAD_SIZE)[:, : GROUP * TILE]
    gathered = gathered.reshape(KEY_VALUE_HEADS, GROUP, TILE, HEAD_SIZE).transpose(0, 2, 1, 3)
    gathered = gathered.reshape(KEY_VALUE_HEADS, TILE, GROUP * HEAD_SIZE)
    result = jnp.zeros((TILE, weight.shape[0]), F32)
    for k, block in enumerate(blocks):
        for f in range(2):
            rows = lax.dynamic_index_in_dim(gathered, (sy ^ k) ^ (Y * f), 0, keepdims=False)
            result = result + lax.dot_general(
                rows, block[f], (((1,), (1,)), ((), ())), preferred_element_type=F32
            )
    return result.astype(BF16)


def solution(mesh):
    return jax.shard_map(
        per_device,
        mesh=mesh,
        in_specs=(
            P("sx", None),
            P(("sx", "sy"), None),
            P(("sx", "sy"), None),
            P(),
            P(("sx", "sy")),
            P("sy", "sx"),
        ),
        out_specs=P("sy", "sx"),
        check_vma=False,
    )
```

time: 134 us -> 108 us (0.81)
  waiting for transfers between devices: 50.5 us -> 27.9 us
  blocking collectives: 0 us -> 15.9 us
  local copies, waits for them, and re-layouts: 16.1 us -> 2.82 us
  starting transfers between devices: 42.1 us -> 34.7 us
    all_to_all x3 -> x2, waiting for transfers between devices: 39.4 us -> 10.9 us  [the longest x1 9.48 us: per_device(): lax.all_to_all(jnp.broadcast_to(attended[None], (size_x, SMALL, HEAD_SIZE...]
    all_to_all x0 -> x1, blocking collectives: none -> 15.9 us  [per_device(): lax.all_to_all(jnp.concatenate([small(out, 0.0), stats], axis=1), ('sx',...]
    all_to_all x3 -> x2, starting transfers between devices: 29.6 us -> 14.6 us  [the longest x1 9.98 us: per_device(): lax.all_to_all(jnp.broadcast_to(attended[None], (size_x, SMALL, HEAD_SIZE...]
    ppermute x8 -> x14, starting transfers between devices: 12.5 us -> 20.1 us  [swap(): return lax.ppermute(a, axis, [(i, i ^ bits) for i in range(size)])]
    ppermute x8 -> x14, waiting for transfers between devices: 11.2 us -> 17 us  [swap(): return lax.ppermute(a, axis, [(i, i ^ bits) for i in range(size)])]
    reshape x5 -> x4, local copies, waits for them, and re-layouts: 5.71 us -> 0.45 us  [the longest x1 0.21 us: per_device(): gathered = gathered.reshape(KEY_VALUE_HEADS, TILE, GROUP * HEAD_SIZE)]
    dynamic_slice x3 -> x0, local copies, waits for them, and re-layouts: 4.79 us -> none  [halves(): return (mine, lax.dynamic_slice_in_dim(a, (1 - core) * width, width, 1))]
    broadcast_in_dim x3 -> x1, local copies, waits for them, and re-layouts: 2.43 us -> 0.71 us  [per_device(): jnp.broadcast_to(attended[None], (size_x, SMALL, HEAD_SIZE))]
  transfers between devices with their start and end apart: 11 -> 16, of which waited for: 5 -> 8; matrix products, arithmetic and copies ran while one was open for 6% -> 3% of each run, Pallas kernels for 0% -> 0%
where the time goes in v2:
time: 108 us; the launch traced here: 107 us
  starting transfers between devices  34.7 us (32%)
  waiting for transfers between devices  27.9 us (26%)
  Pallas kernels  20.4 us (19%)
  blocking collectives  15.9 us (15%)
  local copies, waits for them, and re-layouts  2.82 us (3%)
  matrix products  2.2 us (2%)
  other arithmetic  1.87 us (2%)
  between operations  1.56 us (1%)
    pallas_call x1, Pallas kernels, attend(): pl.pallas_call(attention_kernel, grid_spec=pltpu.PrefetchScalarGridSpec(n...  20.4 us
    ppermute x14, starting transfers between devices, swap(): return lax.ppermute(a, axis, [(i, i ^ bits) for i in range(size)])  20.1 us
    ppermute x14, waiting for transfers between devices, swap(): return lax.ppermute(a, axis, [(i, i ^ bits) for i in range(size)])  17 us
    all_to_all x1, blocking collectives, per_device(): lax.all_to_all(jnp.concatenate([small(out, 0.0), stats], axis=1), ('sx',...  15.9 us
    all_to_all x1, starting transfers between devices, per_device(): lax.all_to_all(jnp.broadcast_to(attended[None], (size_x, SMALL, HEAD_SIZE...  9.98 us
    all_to_all x1, waiting for transfers between devices, per_device(): lax.all_to_all(jnp.broadcast_to(attended[None], (size_x, SMALL, HEAD_SIZE...  9.48 us
    all_to_all x1, starting transfers between devices, per_device(): lax.all_to_all(out.reshape(CHIPS, PIECE + STATS, HEAD_SIZE), ('sx', 'sy')...  4.58 us
    dot_general x8, matrix products, per_device(): lax.dot_general(rows, block[f], (((1,), (1,)), ((), ())), preferred_eleme...  2.2 us
  transfers between devices with their start and end apart: 16, of which 8 were waited for; matrix products, arithmetic and copies ran while one was open for 3% of the time, Pallas kernels for 0%

profile of v2, /device:TPU:1, one launch (start us, length us, event | category | flops | bytes accessed | tf_op | source)
XLA Modules:
  0.0 107.4 jit_solution(15784158755020676307)
XLA Ops:
  0.0 3.2 %collective-permute-start = (bf16[4,5120]{1,0:T(4,128)(2,1)}, bf16[4,5120]{1,0:T(4,128)(2,1)S(1)}, u32[]{:S(2)}, u32[]{:S(2)}) collective-permute-start(bf16[4,5120]{1,0:T(4,128)(2,1)} %param.6), channel_id=1, source_target_pairs={{0,8},{8,0},{16,24},{24,16},{32,40},{40,32},{48,56},{56,48},{64,72... | collective-permute-start | bytes 122888 | tf_op jit(solution)/shard_map/ppermute | solution.py:173
  3.2 1.1 %collective-permute-done = bf16[4,5120]{1,0:T(4,128)(2,1)S(1)} collective-permute-done((bf16[4,5120]{1,0:T(4,128)(2,1)}, bf16[4,5120]{1,0:T(4,128)(2,1)S(1)}, u32[]{:S(2)}, u32[]{:S(2)}) %collective-permute-start) | collective-permute-done | bytes 40992 | tf_op jit(solution)/shard_map/ppermute | solution.py:173
  4.3 0.8 broadcast_select_fusion
  5.1 0.1 fusion.13
  5.2 0.4 collective-permute-start.8
  5.7 0.2 collective-permute-start.9
  5.8 1.3 %collective-permute-start.3 = (bf16[8,2560]{1,0:T(8,128)(2,1)S(1)}, bf16[8,2560]{1,0:T(8,128)(2,1)S(1)}, u32[]{:S(2)}, u32[]{:S(2)}) collective-permute-start(bf16[8,2560]{1,0:T(8,128)(2,1)S(1)} %fusion.13), channel_id=1, source_target_pairs={{0,32},{8,40},{16,48},{24,56},{32,0},{40,8},{48,16},{56,24},{64,96... | collective-permute-start | bytes 122888 | tf_op jit(solution)/shard_map/ppermute | solution.py:173
  7.1 1.4 %collective-permute-start.4 = (bf16[8,2560]{1,0:T(8,128)(2,1)S(1)}, bf16[8,2560]{1,0:T(8,128)(2,1)S(1)}, u32[]{:S(2)}, u32[]{:S(2)}) collective-permute-start(bf16[8,2560]{1,0:T(8,128)(2,1)S(1)} %fusion.13), channel_id=1, source_target_pairs={{0,48},{8,56},{16,32},{24,40},{32,16},{40,24},{48,0},{56,8},{64,11... | collective-permute-start | bytes 122888 | tf_op jit(solution)/shard_map/ppermute | solution.py:173
  8.5 0.3 collective-permute-start.2
  8.7 2.1 %collective-permute-done.3 = bf16[8,2560]{1,0:T(8,128)(2,1)S(1)} collective-permute-done((bf16[8,2560]{1,0:T(8,128)(2,1)S(1)}, bf16[8,2560]{1,0:T(8,128)(2,1)S(1)}, u32[]{:S(2)}, u32[]{:S(2)}) %collective-permute-start.3) | collective-permute-done | bytes 40992 | tf_op jit(solution)/shard_map/ppermute | solution.py:173
  10.9 0.8 collective-permute-start.1
  11.7 0.1 collective-permute-done.4
  11.8 0.0 collective-permute-done.2
  11.9 0.0 copy-start.1
  11.9 1.3 %collective-permute-start.5 = (bf16[32,2560]{1,0:T(8,128)(2,1)S(1)}, bf16[32,2560]{1,0:T(8,128)(2,1)S(1)}, u32[]{:S(2)}, u32[]{:S(2)}) collective-permute-start(bf16[32,2560]{1,0:T(8,128)(2,1)S(1)} %pad_maximum_fusion.2.q0), channel_id=1, source_target_pairs={{0,64},{8,72},{16,80},{24,88},{32,96},{40,104},{48,112},{56,120},{... | collective-permute-start | bytes 491528 | tf_op jit(solution)/shard_map/ppermute | solution.py:173
  13.1 2.5 %collective-permute-start.6 = (bf16[32,2560]{1,0:T(8,128)(2,1)S(1)}, bf16[32,2560]{1,0:T(8,128)(2,1)S(1)}, u32[]{:S(2)}, u32[]{:S(2)}) collective-permute-start(bf16[32,2560]{1,0:T(8,128)(2,1)S(1)} %pad_maximum_fusion.2.q0), channel_id=1, source_target_pairs={{0,128},{8,136},{16,144},{24,152},{32,160},{40,168},{48,176},{56,1... | collective-permute-start | bytes 491528 | tf_op jit(solution)/shard_map/ppermute | solution.py:173
  15.6 3.2 %collective-permute-done.1.valid_pair = s32[1]{0:T(128)} collective-permute-done((s32[1]{0:T(128)}, s32[1]{0:T(128)}, u32[]{:S(2)}, u32[]{:S(2)}) %collective-permute-start.1) | collective-permute-done | bytes 36 | tf_op jit(solution)/shard_map/ppermute | solution.py:173
  18.8 0.7 collective-permute-start.7
  20.9 0.7 stack.58.info
  21.6 0.0 collective-permute-done.5.q1
  21.6 0.0 collective-permute-done.6.q2
  21.6 0.0 copy-start.3
  21.6 5.7 %collective-permute-done.7.q3 = bf16[32,2560]{1,0:T(8,128)(2,1)S(1)} collective-permute-done((bf16[32,2560]{1,0:T(8,128)(2,1)S(1)}, bf16[32,2560]{1,0:T(8,128)(2,1)S(1)}, u32[]{:S(2)}, u32[]{:S(2)}) %collective-permute-start.7) | collective-permute-done | bytes 163872 | tf_op jit(solution)/shard_map/ppermute | solution.py:173
  27.3 0.0 collective-permute-done.8.key_pair
  27.3 0.0 collective-permute-done.9.value_pair
  27.3 0.0 copy-done.1
  27.3 0.0 copy-done.2
  27.3 0.0 copy-done.3
  27.3 0.6 copy-done.4
  28.0 20.4 %shard_map.64 = bf16[4,4,176,128]{3,2,1,0:T(8,128)(2,1)} custom-call(s32[9]{0:T(128)} %stack.58.info, s32[1]{0:T(128)} %collective-permute-done.1.valid_pair, bf16[32,2560]{1,0:T(8,128)(2,1)} %copy-done.1, bf16[32,2560]{1,0:T(8,128)(2,1)} %copy-done.2, bf16[32,2560]{1,0:T(8,128)(2,1)} %copy-done.3, bf16[32,2560]{1,0:T(8,128)(2,1)} %copy-done.4, ...), custom_call_target="tpu_custom_call" | custom-call | flops 10737418240 | bytes 8388608 | tf_op jit(solution)/shard_map/pallas_call | solution.py:124
  48.4 4.6 %all-to-all-start = ((bf16[16,176,128]{2,1,0:T(8,128)(2,1)}), bf16[16,176,128]{2,1,0:T(8,128)(2,1)S(1)}, u32[]{:S(2)}, u32[]{:S(2)}) async-start(bf16[16,176,128]{2,1,0:T(8,128)(2,1)} %bitcast.103), calls=%async_computation | async-start | bytes 1441792 | tf_op jit(solution)/shard_map/all_to_all | solution.py:207
  53.0 0.0 copy-done
  53.0 6.1 %collective-permute-start.10 = (bf16[160,640]{1,0:T(8,128)(2,1)S(1)}, bf16[160,640]{1,0:T(8,128)(2,1)S(1)}, u32[]{:S(2)}, u32[]{:S(2)}) collective-permute-start(bf16[160,640]{1,0:T(8,128)(2,1)S(1)} %bitcast.99), channel_id=1, source_target_pairs={{0,4},{1,5},{2,6},{3,7},{4,0},{5,1},{6,2},{7,3},{8,12},{9,13},{10,... | collective-permute-start | bytes 614408 | tf_op jit(solution)/shard_map/ppermute | solution.py:173
  59.1 4.7 %collective-permute-done.10 = bf16[160,640]{1,0:T(8,128)(2,1)S(1)} collective-permute-done((bf16[160,640]{1,0:T(8,128)(2,1)S(1)}, bf16[160,640]{1,0:T(8,128)(2,1)S(1)}, u32[]{:S(2)}, u32[]{:S(2)}) %collective-permute-start.10) | collective-permute-done | bytes 204832 | tf_op jit(solution)/shard_map/ppermute | solution.py:173
  63.8 1.4 %all-to-all-done = bf16[16,176,128]{2,1,0:T(8,128)(2,1)S(1)} async-done(((bf16[16,176,128]{2,1,0:T(8,128)(2,1)}), bf16[16,176,128]{2,1,0:T(8,128)(2,1)S(1)}, u32[]{:S(2)}, u32[]{:S(2)}) %all-to-all-start) | async-done | bytes 720928 | tf_op jit(solution)/shard_map/all_to_all | solution.py:207
  65.3 0.4 collective-permute-start.11
  65.7 1.2 %collective-permute-start.12 = (bf16[2,160,640]{2,1,0:T(8,128)(2,1)S(1)}, bf16[2,160,640]{2,1,0:T(8,128)(2,1)S(1)}, u32[]{:S(2)}, u32[]{:S(2)}) collective-permute-start(bf16[2,160,640]{2,1,0:T(8,128)(2,1)S(1)} %pad_maximum_fusion), channel_id=1, source_target_pairs={{0,3},{1,2},{2,1},{3,0},{4,7},{5,6},{6,5},{7,4},{8,11},{9,10},{10,... | collective-permute-start | bytes 1228808 | tf_op jit(solution)/shard_map/ppermute | solution.py:173
  66.9 0.2 fusion.35
  67.1 0.1 reshape.85
  67.2 0.4 multiply_reduce_fusion
  67.6 0.1 reshape.86
  67.7 0.1 stack_reshape.7
  67.8 0.1 stack_reshape.6
  68.0 15.9 %all_to_all.15 = f32[8,32,128]{2,1,0:T(8,128)S(1)} all-to-all(f32[8,32,128]{2,1,0:T(8,128)S(1)} %pad_maximum_fusion.3), channel_id=1, replica_groups={{0,16,32,48,4,20,36,52},{1,17,33,49,5,21,37,53},{2,18,34,50,6,22,38,54}..., dimensions={0} | all-to-all | bytes 262144 | tf_op jit(solution)/shard_map/all_to_all | solution.py:230
  83.9 0.0 collective-permute-done.11
  83.9 0.0 collective-permute-done.12
  83.9 0.1 copy.17
  84.0 0.1 multiply_reduce_fusion.1
  84.1 0.1 divide_convert_fusion
  84.2 0.7 broadcast_in_dim.2
  84.9 10.0 %all-to-all-start.2 = ((bf16[32,24,128]{2,1,0:T(8,128)(2,1)}), bf16[32,24,128]{2,1,0:T(8,128)(2,1)S(1)}, u32[]{:S(2)}, u32[]{:S(2)}) async-start(bf16[32,24,128]{2,1,0:T(8,128)(2,1)} %broadcast_in_dim.2), calls=%async_computation.2 | async-start | bytes 393216 | tf_op jit(solution)/shard_map/all_to_all | solution.py:239
  94.9 0.4 collective-permute-start.13
  95.3 9.5 %all-to-all-done.2 = bf16[32,24,128]{2,1,0:T(8,128)(2,1)S(1)} async-done(((bf16[32,24,128]{2,1,0:T(8,128)(2,1)}), bf16[32,24,128]{2,1,0:T(8,128)(2,1)S(1)}, u32[]{:S(2)}, u32[]{:S(2)}) %all-to-all-start.2) | async-done | bytes 196640 | tf_op jit(solution)/shard_map/all_to_all | solution.py:239
  104.8 0.1 copy.25
  104.9 0.2 reshape.90
  105.1 0.1 fusion.21
  105.3 0.2 convolution_add_fusion.4
  105.5 0.2 convolution_add_fusion.3
  105.7 0.2 fusion.5
  105.9 0.2 convolution_add_fusion.2
  106.1 0.0 collective-permute-done.13
  106.1 0.2 fusion.3
  106.3 0.2 fusion.1
  106.5 0.9 fusion.2
  (21 shorter events, 0.3 us)
Async XLA Ops:
  0.0 4.3 %collective-permute-start = (bf16[4,5120]{1,0:T(4,128)(2,1)}, bf16[4,5120]{1,0:T(4,128)(2,1)S(1)}, u32[]{:S(2)}, u32[]{:S(2)}) collective-permute-start(bf16[4,5120]{1,0:T(4,128)(2,1)} %param.6), channel_id=1, source_target_pairs={{0,8},{8,0},{16,24},{24,16},{32,40},{40,32},{48,56},{56,48},{64,72... | collective-permute-start | bytes 122888 | tf_op jit(solution)/shard_map/ppermute | solution.py:173
  5.2 22.1 %collective-permute-start.8 = (bf16[2048,1024]{1,0:T(8,128)(2,1)}, bf16[2048,1024]{1,0:T(8,128)(2,1)}, u32[]{:S(2)}, u32[]{:S(2)}) collective-permute-start(bf16[2048,1024]{1,0:T(8,128)(2,1)} %key_own), channel_id=1, source_target_pairs={{0,8},{8,0},{16,24},{24,16},{32,40},{40,32},{48,56},{56,48},{64,72... | collective-permute-start | bytes 12582920 | tf_op jit(solution)/shard_map/ppermute | solution.py:173
  5.7 21.6 %collective-permute-start.9 = (bf16[2048,1024]{1,0:T(8,128)(2,1)}, bf16[2048,1024]{1,0:T(8,128)(2,1)}, u32[]{:S(2)}, u32[]{:S(2)}) collective-permute-start(bf16[2048,1024]{1,0:T(8,128)(2,1)} %value_own), channel_id=1, source_target_pairs={{0,8},{8,0},{16,24},{24,16},{32,40},{40,32},{48,56},{56,48},{64,72... | collective-permute-start | bytes 12582920 | tf_op jit(solution)/shard_map/ppermute | solution.py:173
  5.8 5.0 %collective-permute-start.3 = (bf16[8,2560]{1,0:T(8,128)(2,1)S(1)}, bf16[8,2560]{1,0:T(8,128)(2,1)S(1)}, u32[]{:S(2)}, u32[]{:S(2)}) collective-permute-start(bf16[8,2560]{1,0:T(8,128)(2,1)S(1)} %fusion.13), channel_id=1, source_target_pairs={{0,32},{8,40},{16,48},{24,56},{32,0},{40,8},{48,16},{56,24},{64,96... | collective-permute-start | bytes 122888 | tf_op jit(solution)/shard_map/ppermute | solution.py:173
  7.1 4.7 %collective-permute-start.4 = (bf16[8,2560]{1,0:T(8,128)(2,1)S(1)}, bf16[8,2560]{1,0:T(8,128)(2,1)S(1)}, u32[]{:S(2)}, u32[]{:S(2)}) collective-permute-start(bf16[8,2560]{1,0:T(8,128)(2,1)S(1)} %fusion.13), channel_id=1, source_target_pairs={{0,48},{8,56},{16,32},{24,40},{32,16},{40,24},{48,0},{56,8},{64,11... | collective-permute-start | bytes 122888 | tf_op jit(solution)/shard_map/ppermute | solution.py:173
  8.5 3.3 %collective-permute-start.2 = (bf16[8,2560]{1,0:T(8,128)(2,1)S(1)}, bf16[8,2560]{1,0:T(8,128)(2,1)S(1)}, u32[]{:S(2)}, u32[]{:S(2)}) collective-permute-start(bf16[8,2560]{1,0:T(8,128)(2,1)S(1)} %fusion.13), channel_id=1, source_target_pairs={{0,16},{8,24},{16,0},{24,8},{32,48},{40,56},{48,32},{56,40},{64,80... | collective-permute-start | bytes 122888 | tf_op jit(solution)/shard_map/ppermute | solution.py:173
  10.9 8.0 %collective-permute-start.1 = (s32[1]{0:T(128)}, s32[1]{0:T(128)}, u32[]{:S(2)}, u32[]{:S(2)}) collective-permute-start(s32[1]{0:T(128)} %param.10), channel_id=1, source_target_pairs={{0,8},{8,0},{16,24},{24,16},{32,40},{40,32},{48,56},{56,48},{64,72... | collective-permute-start | bytes 20 | tf_op jit(solution)/shard_map/ppermute | solution.py:173
  11.9 15.4 %copy-start.1 = (bf16[32,2560]{1,0:T(8,128)(2,1)}, bf16[32,2560]{1,0:T(8,128)(2,1)S(1)}, u32[]{:S(2)}) copy-start(bf16[32,2560]{1,0:T(8,128)(2,1)S(1)} %pad_maximum_fusion.2.q0) | copy-start | bytes 491524
  11.9 9.7 %collective-permute-start.5 = (bf16[32,2560]{1,0:T(8,128)(2,1)S(1)}, bf16[32,2560]{1,0:T(8,128)(2,1)S(1)}, u32[]{:S(2)}, u32[]{:S(2)}) collective-permute-start(bf16[32,2560]{1,0:T(8,128)(2,1)S(1)} %pad_maximum_fusion.2.q0), channel_id=1, source_target_pairs={{0,64},{8,72},{16,80},{24,88},{32,96},{40,104},{48,112},{56,120},{... | collective-permute-start | bytes 491528 | tf_op jit(solution)/shard_map/ppermute | solution.py:173
  13.1 8.4 %collective-permute-start.6 = (bf16[32,2560]{1,0:T(8,128)(2,1)S(1)}, bf16[32,2560]{1,0:T(8,128)(2,1)S(1)}, u32[]{:S(2)}, u32[]{:S(2)}) collective-permute-start(bf16[32,2560]{1,0:T(8,128)(2,1)S(1)} %pad_maximum_fusion.2.q0), channel_id=1, source_target_pairs={{0,128},{8,136},{16,144},{24,152},{32,160},{40,168},{48,176},{56,1... | collective-permute-start | bytes 491528 | tf_op jit(solution)/shard_map/ppermute | solution.py:173
  18.8 8.5 %collective-permute-start.7 = (bf16[32,2560]{1,0:T(8,128)(2,1)S(1)}, bf16[32,2560]{1,0:T(8,128)(2,1)S(1)}, u32[]{:S(2)}, u32[]{:S(2)}) collective-permute-start(bf16[32,2560]{1,0:T(8,128)(2,1)S(1)} %pad_maximum_fusion.2.q0), channel_id=1, source_target_pairs={{0,192},{8,200},{16,208},{24,216},{32,224},{40,232},{48,240},{56,2... | collective-permute-start | bytes 491528 | tf_op jit(solution)/shard_map/ppermute | solution.py:173
  21.6 31.4 %copy-start = (bf16[640,160]{0,1:T(8,128)(2,1)S(1)}, bf16[640,160]{0,1:T(8,128)(2,1)}, u32[]{:S(2)}) copy-start(bf16[640,160]{0,1:T(8,128)(2,1)} %param.11) | copy-start | bytes 614404
  21.6 5.7 %copy-start.2 = (bf16[32,2560]{1,0:T(8,128)(2,1)}, bf16[32,2560]{1,0:T(8,128)(2,1)S(1)}, u32[]{:S(2)}) copy-start(bf16[32,2560]{1,0:T(8,128)(2,1)S(1)} %collective-permute-done.5.q1) | copy-start | bytes 491524
  21.6 5.7 %copy-start.3 = (bf16[32,2560]{1,0:T(8,128)(2,1)}, bf16[32,2560]{1,0:T(8,128)(2,1)S(1)}, u32[]{:S(2)}) copy-start(bf16[32,2560]{1,0:T(8,128)(2,1)S(1)} %collective-permute-done.6.q2) | copy-start | bytes 491524
  27.3 0.7 copy-start.4
  48.4 16.8 %all-to-all-start = ((bf16[16,176,128]{2,1,0:T(8,128)(2,1)}), bf16[16,176,128]{2,1,0:T(8,128)(2,1)S(1)}, u32[]{:S(2)}, u32[]{:S(2)}) async-start(bf16[16,176,128]{2,1,0:T(8,128)(2,1)} %bitcast.103), calls=%async_computation | async-start | bytes 1441792 | tf_op jit(solution)/shard_map/all_to_all | solution.py:207
  53.0 10.8 %collective-permute-start.10 = (bf16[160,640]{1,0:T(8,128)(2,1)S(1)}, bf16[160,640]{1,0:T(8,128)(2,1)S(1)}, u32[]{:S(2)}, u32[]{:S(2)}) collective-permute-start(bf16[160,640]{1,0:T(8,128)(2,1)S(1)} %bitcast.99), channel_id=1, source_target_pairs={{0,4},{1,5},{2,6},{3,7},{4,0},{5,1},{6,2},{7,3},{8,12},{9,13},{10,... | collective-permute-start | bytes 614408 | tf_op jit(solution)/shard_map/ppermute | solution.py:173
  65.3 18.6 %collective-permute-start.11 = (bf16[2,160,640]{2,1,0:T(8,128)(2,1)S(1)}, bf16[2,160,640]{2,1,0:T(8,128)(2,1)S(1)}, u32[]{:S(2)}, u32[]{:S(2)}) collective-permute-start(bf16[2,160,640]{2,1,0:T(8,128)(2,1)S(1)} %pad_maximum_fusion), channel_id=1, source_target_pairs={{0,1},{1,0},{2,3},{3,2},{4,5},{5,4},{6,7},{7,6},{8,9},{9,8},{10,11... | collective-permute-start | bytes 1228808 | tf_op jit(solution)/shard_map/ppermute | solution.py:173
  65.7 18.2 %collective-permute-start.12 = (bf16[2,160,640]{2,1,0:T(8,128)(2,1)S(1)}, bf16[2,160,640]{2,1,0:T(8,128)(2,1)S(1)}, u32[]{:S(2)}, u32[]{:S(2)}) collective-permute-start(bf16[2,160,640]{2,1,0:T(8,128)(2,1)S(1)} %pad_maximum_fusion), channel_id=1, source_target_pairs={{0,3},{1,2},{2,1},{3,0},{4,7},{5,6},{6,5},{7,4},{8,11},{9,10},{10,... | collective-permute-start | bytes 1228808 | tf_op jit(solution)/shard_map/ppermute | solution.py:173
  84.9 19.9 %all-to-all-start.2 = ((bf16[32,24,128]{2,1,0:T(8,128)(2,1)}), bf16[32,24,128]{2,1,0:T(8,128)(2,1)S(1)}, u32[]{:S(2)}, u32[]{:S(2)}) async-start(bf16[32,24,128]{2,1,0:T(8,128)(2,1)} %broadcast_in_dim.2), calls=%async_computation.2 | async-start | bytes 393216 | tf_op jit(solution)/shard_map/all_to_all | solution.py:239
  94.9 11.2 %collective-permute-start.13 = (bf16[2,160,640]{2,1,0:T(8,128)(2,1)S(1)}, bf16[2,160,640]{2,1,0:T(8,128)(2,1)S(1)}, u32[]{:S(2)}, u32[]{:S(2)}) collective-permute-start(bf16[2,160,640]{2,1,0:T(8,128)(2,1)S(1)} %collective-permute-done.12), channel_id=1, source_target_pairs={{0,1},{1,0},{2,3},{3,2},{4,5},{5,4},{6,7},{7,6},{8,9},{9,8},{10,11... | collective-permute-start | bytes 1228808 | tf_op jit(solution)/shard_map/ppermute | solution.py:173

commit v3 on v2

v3 whole, which is shorter than its diff:
```python
import jax
import jax.numpy as jnp
from jax import lax
from jax.experimental import pallas as pl
from jax.experimental.pallas import tpu as pltpu
from jax.sharding import PartitionSpec as P

HQ = 40
KEY_VALUE_HEADS = 8
HEAD_SIZE = 128
GROUP = 5
LOG2E = 1.4426950408889634
BF16 = jnp.bfloat16
F32 = jnp.float32
CHIPS = 16
Y = 4
CORE_HEADS = 4
CHUNK = 1024
TILE = 16
PIECE = 2 * GROUP * TILE
STATS = 16
SMALL = 24


def attention_kernel(
    info, q0, q1, q2, q3, key_own, key_pair, value_own, value_pair, out, bias, lhs, factors
):
    head = pl.program_id(0)
    rows = lhs.shape[0]
    tokens = rows // GROUP
    slots = key_own.shape[0]
    tiles = tokens // TILE

    @pl.when(head == 0)
    def _():
        step = 256
        token = lax.broadcasted_iota(jnp.int32, (1, tokens), 1)
        for source, (limit, base) in enumerate(((info[1], info[2]), (info[5], info[3]))):
            last = jnp.minimum(limit - 1, token - base)

            def fill(i, carry, source=source, last=last):
                entry = lax.broadcasted_iota(jnp.int32, (step, tokens), 0) + i * step
                at = pl.multiple_of(source * slots + i * step, step)
                bias[pl.ds(at, step), :] = jnp.where(entry <= last, 0.0, -1e30).astype(BF16)
                return carry

            lax.fori_loop(0, slots // step, fill, 0, unroll=True)
        place = lax.broadcasted_iota(jnp.int32, (tokens, HEAD_SIZE), 0)
        buckets = ((info[4] + place + 1) >> 13).astype(F32)
        scale = (1.0 + 0.1 * jnp.log(buckets + 1.0)) * (HEAD_SIZE ** (-0.5) * LOG2E)
        row = lax.broadcasted_iota(jnp.int32, (TILE, tokens), 0)
        lane = lax.broadcasted_iota(jnp.int32, (TILE, tokens), 1)
        for slot in range(tiles):
            first = ((slot % 2) * Y + slot // 2) * TILE
            one_hot = (lane == row + first).astype(BF16)
            for g in range(GROUP):
                at = slice((slot * GROUP + g) * TILE, (slot * GROUP + g + 1) * TILE)
                lhs[at, HEAD_SIZE:] = one_hot
                factors[at, :] = scale[first : first + TILE]

    for k, block in enumerate((q0, q1, q2, q3)):
        x = info[6 + k]
        for b in range(2):
            slot = ((x % 2) * 2 + b) * 2 + x // 2
            for g in range(GROUP):
                at = pl.multiple_of((slot * GROUP + g) * TILE, TILE)
                lhs[pl.ds(at, TILE), :HEAD_SIZE] = block[
                    b * TILE : (b + 1) * TILE, g * HEAD_SIZE : (g + 1) * HEAD_SIZE
                ]
    left = lhs[...]
    factor = factors[:, :1]
    chunks = [
        (keys, values, bias, source * slots, start)
        for source, (keys, values) in enumerate(((key_own, value_own), (key_pair, value_pair)))
        for start in range(0, slots, CHUNK)
    ]

    def score(keys, values, bias, offset, start):
        right = jnp.concatenate(
            [keys[start : start + CHUNK, :], bias[offset + start : offset + start + CHUNK, :]], axis=1
        )
        return lax.dot_general(left, right, (((1,), (1,)), ((), ())), preferred_element_type=F32)

    peak, following = None, score(*chunks[0])
    for i, (_, values, _, _, start) in enumerate(chunks):
        scores = following
        if i + 1 < len(chunks):
            following = score(*chunks[i + 1])
        top = jnp.max(scores, axis=1, keepdims=True)
        new_peak = top if peak is None else jnp.maximum(peak, top)
        weights = jnp.exp2((scores - new_peak) * factor).astype(BF16)
        both = jnp.concatenate(
            [values[start : start + CHUNK, :], jnp.ones((CHUNK, HEAD_SIZE), BF16)], axis=1
        )
        part = jnp.dot(weights, both, preferred_element_type=F32)
        total = part if peak is None else total * jnp.exp2((peak - new_peak) * factor) + part
        peak = new_peak
    lane = lax.broadcasted_iota(jnp.int32, (rows, HEAD_SIZE), 1)
    rest_m = jnp.broadcast_to(peak * factor, (rows, HEAD_SIZE))
    rest_l = total[:, HEAD_SIZE:]
    packed = jnp.zeros((rows, HEAD_SIZE), F32)
    for k in range(3):
        term_m = rest_m.astype(BF16).astype(F32)
        term_l = rest_l.astype(BF16).astype(F32)
        packed = jnp.where(lane == k, term_m, jnp.where(lane == 3 + k, term_l, packed))
        rest_m, rest_l = rest_m - term_m, rest_l - term_l
    packed = packed.astype(BF16)
    pick = (
        lax.broadcasted_iota(jnp.int32, (8, HEAD_SIZE), 0)
        == lax.broadcasted_iota(jnp.int32, (8, HEAD_SIZE), 1)
    ).astype(BF16)
    for y in range(Y):
        at = slice(y * PIECE, (y + 1) * PIECE)
        out[0, y, :PIECE, :] = total[at, :HEAD_SIZE].astype(BF16)
        turned = lax.dot_general(
            pick, packed[at, :], (((1,), (1,)), ((), ())), preferred_element_type=F32
        )
        second = jnp.concatenate(
            [turned[:, HEAD_SIZE:], jnp.zeros((8, 2 * HEAD_SIZE - PIECE), F32)], axis=1
        )
        out[0, y, PIECE:, :] = jnp.concatenate([turned[:, :HEAD_SIZE], second], axis=0).astype(BF16)


def attend(info, queries, keys, values, key_pair, value_pair):
    tokens = queries[0].shape[0] * 4
    slots = keys.shape[0]
    rows = tokens * GROUP
    cache = pl.BlockSpec((slots, HEAD_SIZE), lambda h, s: (0, s[0] * CORE_HEADS + h))
    quarter = pl.BlockSpec((tokens // 4, GROUP * HEAD_SIZE), lambda h, s: (0, h))
    return pl.pallas_call(
        attention_kernel,
        grid_spec=pltpu.PrefetchScalarGridSpec(
            num_scalar_prefetch=1,
            grid=(CORE_HEADS,),
            in_specs=[
                quarter,
                quarter,
                quarter,
                quarter,
                cache,
                cache,
                cache,
                cache,
            ],
            out_specs=pl.BlockSpec((1, Y, PIECE + STATS, HEAD_SIZE), lambda h, s: (h, 0, 0, 0)),
            scratch_shapes=[
                pltpu.VMEM((2 * slots, tokens), BF16),
                pltpu.VMEM((rows, 2 * HEAD_SIZE), BF16),
                pltpu.VMEM((rows, HEAD_SIZE), F32),
            ],
        ),
        out_shape=jax.ShapeDtypeStruct((CORE_HEADS, Y, PIECE + STATS, HEAD_SIZE), BF16),
        compiler_params=pltpu.CompilerParams(vmem_limit_bytes=60 * 2**20),
        cost_estimate=pl.CostEstimate(
            flops=2 * 2 * CORE_HEADS * rows * 2 * slots * 2 * HEAD_SIZE,
            bytes_accessed=2 * 2 * CORE_HEADS * 2 * slots * HEAD_SIZE,
            transcendentals=CORE_HEADS * rows * 2 * slots,
        ),
    )(info, *queries, keys, key_pair, values, value_pair)


def merge(out, peak, total):
    top = jnp.max(peak, axis=0)
    share = jnp.exp2(peak - top)
    return jnp.sum(out * share[..., None], axis=0), top, jnp.sum(share * total, axis=0)


def per_device(queries, keys, values, opening, valid, weight):
    sx, sy = lax.axis_index("sx"), lax.axis_index("sy")
    size_x, size_y = lax.axis_size("sx"), lax.axis_size("sy")
    core, z_lo, x = sx % 2, (sx // 2) % 4, sx // 8
    own_rows = queries.shape[0]
    tokens = own_rows * size_x
    slots = keys.shape[0]
    half = CORE_HEADS * GROUP * HEAD_SIZE

    def swap(a, axis, bits):
        size = lax.axis_size(axis)
        return lax.ppermute(a, axis, [(i, i ^ bits) for i in range(size)])

    got = swap(queries, "sx", 1)
    chip_rows = jnp.concatenate(
        [jnp.where(core == 0, queries, got), jnp.where(core == 0, got, queries)], axis=0
    )
    chip_rows = lax.dynamic_slice_in_dim(chip_rows, core * half, half, 1)
    valid_pair = swap(valid, "sx", 1)
    chip_rows, keys, values, valid_pair = lax.optimization_barrier((chip_rows, keys, values, valid_pair))
    line = jnp.stack([chip_rows] + [swap(chip_rows, "sx", 2 * k) for k in (1, 2, 3)])
    line = jnp.concatenate(
        [lax.dynamic_index_in_dim(line, z_lo ^ k, 0, keepdims=False) for k in range(4)], axis=0
    )
    line, weight = lax.optimization_barrier((line, weight.T))
    far = swap(weight, "sy", Y)
    all_queries = [line] + [swap(line, "sx", 8 * k) for k in (1, 2, 3)]

    key_pair = swap(keys, "sx", 1)
    value_pair = swap(values, "sx", 1)

    base = (sx * size_y + sy) * slots - opening[0]
    base_pair = ((sx ^ 1) * size_y + sy) * slots - opening[0]
    info = jnp.stack(
        [core, valid[0], base, base_pair, opening[0], valid_pair[0]] + [x ^ k for k in range(4)]
    ).astype(jnp.int32)
    out = attend(info, all_queries, keys, values, key_pair, value_pair)
    out, far = lax.optimization_barrier((out, far))

    def device(x, z_lo, core, z_hi, y):
        return ((x * 4 + z_lo) * 2 + core) * size_y + z_hi * Y + y

    four, two = range(4), range(2)
    planes = [
        [device(x, z, c, h, y) for x in four for y in four] for z in four for c in two for h in two
    ]
    received = lax.all_to_all(
        out.reshape(CHIPS, PIECE + STATS, HEAD_SIZE),
        ("sx", "sy"), 0, 0, tiled=True, axis_index_groups=planes,
    )
    received, far = lax.optimization_barrier((received, far))
    near = jnp.stack([weight, far])
    near_1, near_3 = swap(near, "sy", 1), swap(near, "sy", 3)
    terms = received[:, PIECE:].astype(F32).reshape(CHIPS, 2, 8, HEAD_SIZE)
    peak = (terms[:, :, 0] + (terms[:, :, 1] + terms[:, :, 2])).reshape(CHIPS, -1)[:, :PIECE]
    total = (terms[:, :, 3] + (terms[:, :, 4] + terms[:, :, 5])).reshape(CHIPS, -1)[:, :PIECE]
    out, peak, total = merge(received[:, :PIECE].astype(F32), peak, total)

    rows = PIECE // 2

    def wide(a):
        return jnp.pad(a.reshape(2, 1, rows), ((0, 0), (0, 0), (0, HEAD_SIZE - rows)))

    stats = jnp.concatenate([wide(peak), wide(total), jnp.zeros((2, 6, HEAD_SIZE), F32)], axis=1)
    pieces = jnp.concatenate([out.reshape(2, rows, HEAD_SIZE), stats], axis=1)
    pieces = jnp.broadcast_to(pieces[:, None], (2, 4, rows + 8, HEAD_SIZE))
    lines = [
        [device(x, z, c, h, y) for h in two for z in four] for x in four for c in two for y in four
    ]
    received = lax.all_to_all(
        pieces.reshape(size_y, rows + 8, HEAD_SIZE),
        ("sx", "sy"), 0, 0, tiled=True, axis_index_groups=lines,
    )
    received, near_1, near_3 = lax.optimization_barrier((received, near_1, near_3))
    near_2 = [swap(near_1[0], "sy", 3), swap(near_3[1], "sy", 1)]
    blocks = [near, near_1, near_2, near_3]
    out, _, total = merge(received[:, :rows], received[:, rows, :rows], received[:, rows + 1, :rows])
    attended = (out / total[:, None]).astype(BF16)

    got = swap(attended, "sx", 1)
    both = jnp.stack([jnp.where(core == 0, attended, got), jnp.where(core == 0, got, attended)])
    rings = [[(i * 4 + z) * 2 + c for i in four] for z in four for c in two]
    gathered = lax.all_to_all(
        jnp.broadcast_to(both[None], (4, 2, rows, HEAD_SIZE)), "sx", 0, 0, tiled=True, axis_index_groups=rings
    )
    gathered = gathered.reshape(4, 2, GROUP, TILE, HEAD_SIZE).transpose(1, 0, 3, 2, 4)
    gathered = gathered.reshape(KEY_VALUE_HEADS, TILE, GROUP * HEAD_SIZE)
    result = jnp.zeros((TILE, weight.shape[0]), F32)
    for k, block in enumerate(blocks):
        for f in range(2):
            left = lax.dynamic_index_in_dim(gathered, (sy ^ k) ^ (Y * f), 0, keepdims=False)
            result = result + lax.dot_general(
                left, block[f], (((1,), (1,)), ((), ())), preferred_element_type=F32
            )
    return result.astype(BF16)


def solution(mesh):
    return jax.shard_map(
        per_device,
        mesh=mesh,
        in_specs=(
            P("sx", None),
            P(("sx", "sy"), None),
            P(("sx", "sy"), None),
            P(),
            P(("sx", "sy")),
            P("sy", "sx"),
        ),
        out_specs=P("sy", "sx"),
        check_vma=False,
    )
```

time: 108 us -> 97.1 us (0.90)
  blocking collectives: 15.9 us -> 0 us
  starting transfers between devices: 34.7 us -> 39.4 us
  Pallas kernels: 20.4 us -> 17.5 us
  waiting for transfers between devices: 27.9 us -> 29.8 us
  local copies, waits for them, and re-layouts: 2.82 us -> 4.09 us
    all_to_all x1 -> x0, blocking collectives: 15.9 us -> none  [per_device(): lax.all_to_all(jnp.concatenate([small(out, 0.0), stats], axis=1), ('sx',...]
    all_to_all x1, waiting for transfers between devices: 1.41 us -> 10.5 us  [per_device(): lax.all_to_all(out.reshape(CHIPS, PIECE + STATS, HEAD_SIZE), ('sx', 'sy')...]
    ppermute x14 -> x16, waiting for transfers between devices: 17 us -> 13.3 us  [swap(): return lax.ppermute(a, axis, [(i, i ^ bits) for i in range(size)])]
    all_to_all x1 -> x2, waiting for transfers between devices: 9.48 us -> 5.99 us  [the longest x1 4.3 us: per_device(): lax.all_to_all(jnp.broadcast_to(both[None], (4, 2, rows, HEAD_SIZE)), 'sx...]
    ppermute x14 -> x16, starting transfers between devices: 20.1 us -> 23.4 us  [swap(): return lax.ppermute(a, axis, [(i, i ^ bits) for i in range(size)])]
    pallas_call x1, Pallas kernels: 20.4 us -> 17.5 us  [attend(): pl.pallas_call(attention_kernel, grid_spec=pltpu.PrefetchScalarGridSpec(n...]
    all_to_all x1, starting transfers between devices: 4.58 us -> 6.5 us  [per_device(): lax.all_to_all(out.reshape(CHIPS, PIECE + STATS, HEAD_SIZE), ('sx', 'sy')...]
    all_to_all x1 -> x2, starting transfers between devices: 9.98 us -> 9.56 us  [the longest x1 6.21 us: per_device(): lax.all_to_all(pieces.reshape(size_y, rows + 8, HEAD_SIZE), ('sx', 'sy'),...]
  transfers between devices with their start and end apart: 16 -> 19, of which waited for: 8 -> 10; matrix products, arithmetic and copies ran while one was open for 3% -> 5% of each run, Pallas kernels for 0% -> 18%
where the time goes in v3:
time: 97.1 us; the launch traced here: 96.6 us
  starting transfers between devices  39.4 us (41%)
  waiting for transfers between devices  29.8 us (31%)
  Pallas kernels  17.5 us (18%)
  local copies, waits for them, and re-layouts  4.09 us (4%)
  matrix products  2.16 us (2%)
  other arithmetic  2.08 us (2%)
  between operations  1.54 us (2%)
    ppermute x16, starting transfers between devices, swap(): return lax.ppermute(a, axis, [(i, i ^ bits) for i in range(size)])  23.4 us
    pallas_call x1, Pallas kernels, attend(): pl.pallas_call(attention_kernel, grid_spec=pltpu.PrefetchScalarGridSpec(n...  17.5 us
    ppermute x16, waiting for transfers between devices, swap(): return lax.ppermute(a, axis, [(i, i ^ bits) for i in range(size)])  13.3 us
    all_to_all x1, waiting for transfers between devices, per_device(): lax.all_to_all(out.reshape(CHIPS, PIECE + STATS, HEAD_SIZE), ('sx', 'sy')...  10.5 us
    all_to_all x1, starting transfers between devices, per_device(): lax.all_to_all(out.reshape(CHIPS, PIECE + STATS, HEAD_SIZE), ('sx', 'sy')...  6.5 us
    all_to_all x1, starting transfers between devices, per_device(): lax.all_to_all(pieces.reshape(size_y, rows + 8, HEAD_SIZE), ('sx', 'sy'),...  6.21 us
    all_to_all x1, waiting for transfers between devices, per_device(): lax.all_to_all(jnp.broadcast_to(both[None], (4, 2, rows, HEAD_SIZE)), 'sx...  4.3 us
    all_to_all x1, starting transfers between devices, per_device(): lax.all_to_all(jnp.broadcast_to(both[None], (4, 2, rows, HEAD_SIZE)), 'sx...  3.34 us
  transfers between devices with their start and end apart: 19, of which 10 were waited for; matrix products, arithmetic and copies ran while one was open for 5% of the time, Pallas kernels for 18%

profile of v3, /device:TPU:1, one launch (start us, length us, event | category | flops | bytes accessed | tf_op | source)
XLA Modules:
  0.0 96.6 jit_solution(12056815314567047697)
XLA Ops:
  0.0 3.2 %collective-permute-start = (bf16[4,5120]{1,0:T(4,128)(2,1)}, bf16[4,5120]{1,0:T(4,128)(2,1)S(1)}, u32[]{:S(2)}, u32[]{:S(2)}) collective-permute-start(bf16[4,5120]{1,0:T(4,128)(2,1)} %param.6), channel_id=1, source_target_pairs={{0,8},{8,0},{16,24},{24,16},{32,40},{40,32},{48,56},{56,48},{64,72... | collective-permute-start | bytes 122888 | tf_op jit(solution)/shard_map/ppermute | solution.py:179
  3.2 0.0 collective-permute-start.1
  3.2 1.1 %collective-permute-done = bf16[4,5120]{1,0:T(4,128)(2,1)S(1)} collective-permute-done((bf16[4,5120]{1,0:T(4,128)(2,1)}, bf16[4,5120]{1,0:T(4,128)(2,1)S(1)}, u32[]{:S(2)}, u32[]{:S(2)}) %collective-permute-start) | collective-permute-done | bytes 40992 | tf_op jit(solution)/shard_map/ppermute | solution.py:179
  4.3 0.8 broadcast_select_fusion
  5.1 0.1 fusion.11
  5.2 0.0 collective-permute-done.1
  5.3 0.4 collective-permute-start.8
  5.7 0.2 collective-permute-start.9
  5.9 1.3 %collective-permute-start.3 = (bf16[8,2560]{1,0:T(8,128)(2,1)S(1)}, bf16[8,2560]{1,0:T(8,128)(2,1)S(1)}, u32[]{:S(2)}, u32[]{:S(2)}) collective-permute-start(bf16[8,2560]{1,0:T(8,128)(2,1)S(1)} %fusion.11), channel_id=1, source_target_pairs={{0,32},{8,40},{16,48},{24,56},{32,0},{40,8},{48,16},{56,24},{64,96... | collective-permute-start | bytes 122888 | tf_op jit(solution)/shard_map/ppermute | solution.py:179
  7.1 1.4 %collective-permute-start.4 = (bf16[8,2560]{1,0:T(8,128)(2,1)S(1)}, bf16[8,2560]{1,0:T(8,128)(2,1)S(1)}, u32[]{:S(2)}, u32[]{:S(2)}) collective-permute-start(bf16[8,2560]{1,0:T(8,128)(2,1)S(1)} %fusion.11), channel_id=1, source_target_pairs={{0,48},{8,56},{16,32},{24,40},{32,16},{40,24},{48,0},{56,8},{64,11... | collective-permute-start | bytes 122888 | tf_op jit(solution)/shard_map/ppermute | solution.py:179
  8.5 0.3 collective-permute-start.2
  8.8 2.1 %collective-permute-done.3 = bf16[8,2560]{1,0:T(8,128)(2,1)S(1)} collective-permute-done((bf16[8,2560]{1,0:T(8,128)(2,1)S(1)}, bf16[8,2560]{1,0:T(8,128)(2,1)S(1)}, u32[]{:S(2)}, u32[]{:S(2)}) %collective-permute-start.3) | collective-permute-done | bytes 40992 | tf_op jit(solution)/shard_map/ppermute | solution.py:179
  10.9 0.9 collective-permute-done.4
  11.8 0.0 collective-permute-done.2
  11.9 1.3 %collective-permute-start.5 = (bf16[32,2560]{1,0:T(8,128)(2,1)S(1)}, bf16[32,2560]{1,0:T(8,128)(2,1)S(1)}, u32[]{:S(2)}, u32[]{:S(2)}) collective-permute-start(bf16[32,2560]{1,0:T(8,128)(2,1)S(1)} %pad_maximum_fusion.2.q0), channel_id=1, source_target_pairs={{0,64},{8,72},{16,80},{24,88},{32,96},{40,104},{48,112},{56,120},{... | collective-permute-start | bytes 491528 | tf_op jit(solution)/shard_map/ppermute | solution.py:179
  13.2 2.5 %collective-permute-start.6 = (bf16[32,2560]{1,0:T(8,128)(2,1)S(1)}, bf16[32,2560]{1,0:T(8,128)(2,1)S(1)}, u32[]{:S(2)}, u32[]{:S(2)}) collective-permute-start(bf16[32,2560]{1,0:T(8,128)(2,1)S(1)} %pad_maximum_fusion.2.q0), channel_id=1, source_target_pairs={{0,128},{8,136},{16,144},{24,152},{32,160},{40,168},{48,176},{56,1... | collective-permute-start | bytes 491528 | tf_op jit(solution)/shard_map/ppermute | solution.py:179
  15.6 0.2 collective-permute-start.7
  17.2 1.3 %stack.64.info = s32[10]{0:T(128)} concatenate(s32[1]{0:T(128)} %bitcast, s32[1]{0:T(128)S(6)} %copy.25, s32[1]{0:T(128)} %bitcast.2, s32[1]{0:T(128)} %bitcast.3, s32[1]{0:T(128)} %copy.24, s32[1]{0:T(128)} %collective-permute-done.1, s32[1]{0:T(128)} %bitcast.4, s32[1]{0:T(128)} %bitcast.5, s32[1]{0:T(128)} %bitcast.6, s32[1]{0:T(128)} %bitcast.7), dimensions={0} | concatenate | bytes 80 | tf_op jit(solution)/shard_map/stack | solution.py:201
  18.5 0.0 collective-permute-done.5.q1
  18.5 5.8 %collective-permute-start.10 = (bf16[160,640]{1,0:T(8,128)(2,1)}, bf16[160,640]{1,0:T(8,128)(2,1)S(1)}, u32[]{:S(2)}, u32[]{:S(2)}) collective-permute-start(bf16[160,640]{1,0:T(8,128)(2,1)} %bitcast.93), channel_id=1, source_target_pairs={{0,4},{1,5},{2,6},{3,7},{4,0},{5,1},{6,2},{7,3},{8,12},{9,13},{10,... | collective-permute-start | bytes 614408 | tf_op jit(solution)/shard_map/ppermute | solution.py:179
  24.2 0.0 collective-permute-done.6.q2
  24.3 0.0 collective-permute-done.7.q3
  24.3 0.6 copy-done.3
  24.9 0.1 copy-done.4
  25.0 17.5 %shard_map.64 = bf16[4,4,176,128]{3,2,1,0:T(8,128)(2,1)} custom-call(s32[10]{0:T(128)} %stack.64.info, bf16[32,2560]{1,0:T(8,128)(2,1)} %copy-done.1, bf16[32,2560]{1,0:T(8,128)(2,1)} %copy-done.2, bf16[32,2560]{1,0:T(8,128)(2,1)} %copy-done.3, bf16[32,2560]{1,0:T(8,128)(2,1)} %copy-done.4, bf16[2048,1024]{1,0:T(8,128)(2,1)} %key_own, ...), custom_call_target="tpu_custom_call" | custom-call | flops 10737418240 | bytes 8388608 | tf_op jit(solution)/shard_map/pallas_call | solution.py:130
  42.5 0.0 collective-permute-done.10
  42.5 6.5 %all-to-all-start = ((bf16[16,176,128]{2,1,0:T(8,128)(2,1)}), bf16[16,176,128]{2,1,0:T(8,128)(2,1)S(1)}, u32[]{:S(2)}, u32[]{:S(2)}) async-start(bf16[16,176,128]{2,1,0:T(8,128)(2,1)} %bitcast.96), calls=%async_computation | async-start | bytes 1441792 | tf_op jit(solution)/shard_map/all_to_all | solution.py:214
  49.0 0.1 pad.16.clone
  49.1 10.5 %all-to-all-done = bf16[16,176,128]{2,1,0:T(8,128)(2,1)S(1)} async-done(((bf16[16,176,128]{2,1,0:T(8,128)(2,1)}), bf16[16,176,128]{2,1,0:T(8,128)(2,1)S(1)}, u32[]{:S(2)}, u32[]{:S(2)}) %all-to-all-start) | async-done | bytes 720928 | tf_op jit(solution)/shard_map/all_to_all | solution.py:214
  59.6 0.2 fusion.34
  59.8 0.1 reshape.66
  59.9 0.4 multiply_reduce_fusion
  60.3 0.1 reshape.67
  60.4 0.1 fusion.8
  60.5 0.8 broadcast_in_dim.7
  61.2 6.2 %all-to-all-start.1 = ((f32[8,88,128]{2,1,0:T(8,128)}), f32[8,88,128]{2,1,0:T(8,128)S(1)}, u32[]{:S(2)}, u32[]{:S(2)}) async-start(f32[8,88,128]{2,1,0:T(8,128)} %bitcast.21), calls=%async_computation.1 | async-start | bytes 720896 | tf_op jit(solution)/shard_map/all_to_all | solution.py:237
  67.5 0.4 collective-permute-start.11
  67.9 0.8 collective-permute-start.12
  68.7 6.4 %collective-permute-done.11 = bf16[2,160,640]{2,1,0:T(8,128)(2,1)S(1)} collective-permute-done((bf16[2,160,640]{2,1,0:T(8,128)(2,1)S(1)}, bf16[2,160,640]{2,1,0:T(8,128)(2,1)S(1)}, u32[]{:S(2)}, u32[]{:S(2)}) %collective-permute-start.11) | collective-permute-done | bytes 409632 | tf_op jit(solution)/shard_map/ppermute | solution.py:179
  75.0 1.2 %collective-permute-done.12 = bf16[2,160,640]{2,1,0:T(8,128)(2,1)S(1)} collective-permute-done((bf16[2,160,640]{2,1,0:T(8,128)(2,1)S(1)}, bf16[2,160,640]{2,1,0:T(8,128)(2,1)S(1)}, u32[]{:S(2)}, u32[]{:S(2)}) %collective-permute-start.12) | collective-permute-done | bytes 409632 | tf_op jit(solution)/shard_map/ppermute | solution.py:179
  76.3 1.7 %all-to-all-done.1 = f32[8,88,128]{2,1,0:T(8,128)S(1)} async-done(((f32[8,88,128]{2,1,0:T(8,128)}), f32[8,88,128]{2,1,0:T(8,128)S(1)}, u32[]{:S(2)}, u32[]{:S(2)}) %all-to-all-start.1) | async-done | bytes 360480 | tf_op jit(solution)/shard_map/all_to_all | solution.py:237
  78.0 0.1 copy.18
  78.1 0.2 multiply_reduce_fusion.1
  78.2 0.1 divide_convert_fusion
  78.3 4.6 %collective-permute-start.13 = (bf16[80,128]{1,0:T(8,128)(2,1)S(1)}, bf16[80,128]{1,0:T(8,128)(2,1)S(1)}, u32[]{:S(2)}, u32[]{:S(2)}) collective-permute-start(bf16[80,128]{1,0:T(8,128)(2,1)S(1)} %divide_convert_fusion), channel_id=1, source_target_pairs={{0,8},{8,0},{16,24},{24,16},{32,40},{40,32},{48,56},{56,48},{64,72... | collective-permute-start | bytes 61448 | tf_op jit(solution)/shard_map/ppermute | solution.py:179
  83.0 0.4 collective-permute-start.15
  83.4 0.5 collective-permute-done.13
  83.8 0.1 select_bitcast_fusion.1
  83.9 0.7 broadcast_in_dim.8
  84.6 3.3 %all-to-all-start.2 = ((bf16[4,2,80,128]{3,2,1,0:T(8,128)(2,1)}), bf16[4,2,80,128]{3,2,1,0:T(8,128)(2,1)S(1)}, u32[]{:S(2)}, u32[]{:S(2)}) async-start(bf16[4,2,80,128]{3,2,1,0:T(8,128)(2,1)} %broadcast_in_dim.8), calls=%async_computation.2 | async-start | bytes 327680 | tf_op jit(solution)/shard_map/all_to_all | solution.py:250
  88.0 0.7 collective-permute-start.14
  88.7 4.3 %all-to-all-done.2 = bf16[4,2,80,128]{3,2,1,0:T(8,128)(2,1)S(1)} async-done(((bf16[4,2,80,128]{3,2,1,0:T(8,128)(2,1)}), bf16[4,2,80,128]{3,2,1,0:T(8,128)(2,1)S(1)}, u32[]{:S(2)}, u32[]{:S(2)}) %all-to-all-start.2) | async-done | bytes 163872 | tf_op jit(solution)/shard_map/all_to_all | solution.py:250
  93.0 0.1 copy.19
  93.1 0.2 reshape.70
  93.3 0.1 fusion.20
  93.4 0.2 convolution_add_fusion.4
  93.7 0.2 convolution_add_fusion.3
  93.9 0.2 convolution_add_fusion.2
  94.1 0.2 fusion.3
  94.3 0.0 collective-permute-done.15
  94.3 0.2 fusion.14
  94.5 1.1 %collective-permute-done.14 = bf16[160,640]{1,0:T(8,128)(2,1)S(1)} collective-permute-done((bf16[160,640]{1,0:T(8,128)(2,1)S(1)}, bf16[160,640]{1,0:T(8,128)(2,1)S(1)}, u32[]{:S(2)}, u32[]{:S(2)}) %collective-permute-start.14) | collective-permute-done | bytes 204832 | tf_op jit(solution)/shard_map/ppermute | solution.py:179
  95.6 0.1 fusion.1
  95.7 0.9 fusion.2
  (25 shorter events, 0.3 us)
Async XLA Ops:
  0.0 4.3 %collective-permute-start = (bf16[4,5120]{1,0:T(4,128)(2,1)}, bf16[4,5120]{1,0:T(4,128)(2,1)S(1)}, u32[]{:S(2)}, u32[]{:S(2)}) collective-permute-start(bf16[4,5120]{1,0:T(4,128)(2,1)} %param.6), channel_id=1, source_target_pairs={{0,8},{8,0},{16,24},{24,16},{32,40},{40,32},{48,56},{56,48},{64,72... | collective-permute-start | bytes 122888 | tf_op jit(solution)/shard_map/ppermute | solution.py:179
  3.2 2.0 %collective-permute-start.1 = (s32[1]{0:T(128)}, s32[1]{0:T(128)}, u32[]{:S(2)}, u32[]{:S(2)}) collective-permute-start(s32[1]{0:T(128)} %param.10), channel_id=1, source_target_pairs={{0,8},{8,0},{16,24},{24,16},{32,40},{40,32},{48,56},{56,48},{64,72... | collective-permute-start | bytes 20 | tf_op jit(solution)/shard_map/ppermute | solution.py:179
  5.3 19.0 %collective-permute-start.8 = (bf16[2048,1024]{1,0:T(8,128)(2,1)}, bf16[2048,1024]{1,0:T(8,128)(2,1)}, u32[]{:S(2)}, u32[]{:S(2)}) collective-permute-start(bf16[2048,1024]{1,0:T(8,128)(2,1)} %key_own), channel_id=1, source_target_pairs={{0,8},{8,0},{16,24},{24,16},{32,40},{40,32},{48,56},{56,48},{64,72... | collective-permute-start | bytes 12582920 | tf_op jit(solution)/shard_map/ppermute | solution.py:179
  5.7 18.6 %collective-permute-start.9 = (bf16[2048,1024]{1,0:T(8,128)(2,1)}, bf16[2048,1024]{1,0:T(8,128)(2,1)}, u32[]{:S(2)}, u32[]{:S(2)}) collective-permute-start(bf16[2048,1024]{1,0:T(8,128)(2,1)} %value_own), channel_id=1, source_target_pairs={{0,8},{8,0},{16,24},{24,16},{32,40},{40,32},{48,56},{56,48},{64,72... | collective-permute-start | bytes 12582920 | tf_op jit(solution)/shard_map/ppermute | solution.py:179
  5.9 5.0 %collective-permute-start.3 = (bf16[8,2560]{1,0:T(8,128)(2,1)S(1)}, bf16[8,2560]{1,0:T(8,128)(2,1)S(1)}, u32[]{:S(2)}, u32[]{:S(2)}) collective-permute-start(bf16[8,2560]{1,0:T(8,128)(2,1)S(1)} %fusion.11), channel_id=1, source_target_pairs={{0,32},{8,40},{16,48},{24,56},{32,0},{40,8},{48,16},{56,24},{64,96... | collective-permute-start | bytes 122888 | tf_op jit(solution)/shard_map/ppermute | solution.py:179
  7.1 4.7 %collective-permute-start.4 = (bf16[8,2560]{1,0:T(8,128)(2,1)S(1)}, bf16[8,2560]{1,0:T(8,128)(2,1)S(1)}, u32[]{:S(2)}, u32[]{:S(2)}) collective-permute-start(bf16[8,2560]{1,0:T(8,128)(2,1)S(1)} %fusion.11), channel_id=1, source_target_pairs={{0,48},{8,56},{16,32},{24,40},{32,16},{40,24},{48,0},{56,8},{64,11... | collective-permute-start | bytes 122888 | tf_op jit(solution)/shard_map/ppermute | solution.py:179
  8.5 3.3 %collective-permute-start.2 = (bf16[8,2560]{1,0:T(8,128)(2,1)S(1)}, bf16[8,2560]{1,0:T(8,128)(2,1)S(1)}, u32[]{:S(2)}, u32[]{:S(2)}) collective-permute-start(bf16[8,2560]{1,0:T(8,128)(2,1)S(1)} %fusion.11), channel_id=1, source_target_pairs={{0,16},{8,24},{16,0},{24,8},{32,48},{40,56},{48,32},{56,40},{64,80... | collective-permute-start | bytes 122888 | tf_op jit(solution)/shard_map/ppermute | solution.py:179
  11.9 12.4 %copy-start.1 = (bf16[32,2560]{1,0:T(8,128)(2,1)}, bf16[32,2560]{1,0:T(8,128)(2,1)S(1)}, u32[]{:S(2)}) copy-start(bf16[32,2560]{1,0:T(8,128)(2,1)S(1)} %pad_maximum_fusion.2.q0) | copy-start | bytes 491524
  11.9 6.6 %collective-permute-start.5 = (bf16[32,2560]{1,0:T(8,128)(2,1)S(1)}, bf16[32,2560]{1,0:T(8,128)(2,1)S(1)}, u32[]{:S(2)}, u32[]{:S(2)}) collective-permute-start(bf16[32,2560]{1,0:T(8,128)(2,1)S(1)} %pad_maximum_fusion.2.q0), channel_id=1, source_target_pairs={{0,64},{8,72},{16,80},{24,88},{32,96},{40,104},{48,112},{56,120},{... | collective-permute-start | bytes 491528 | tf_op jit(solution)/shard_map/ppermute | solution.py:179
  13.2 11.1 %collective-permute-start.6 = (bf16[32,2560]{1,0:T(8,128)(2,1)S(1)}, bf16[32,2560]{1,0:T(8,128)(2,1)S(1)}, u32[]{:S(2)}, u32[]{:S(2)}) collective-permute-start(bf16[32,2560]{1,0:T(8,128)(2,1)S(1)} %pad_maximum_fusion.2.q0), channel_id=1, source_target_pairs={{0,128},{8,136},{16,144},{24,152},{32,160},{40,168},{48,176},{56,1... | collective-permute-start | bytes 491528 | tf_op jit(solution)/shard_map/ppermute | solution.py:179
  15.6 8.7 %collective-permute-start.7 = (bf16[32,2560]{1,0:T(8,128)(2,1)S(1)}, bf16[32,2560]{1,0:T(8,128)(2,1)S(1)}, u32[]{:S(2)}, u32[]{:S(2)}) collective-permute-start(bf16[32,2560]{1,0:T(8,128)(2,1)S(1)} %pad_maximum_fusion.2.q0), channel_id=1, source_target_pairs={{0,192},{8,200},{16,208},{24,216},{32,224},{40,232},{48,240},{56,2... | collective-permute-start | bytes 491528 | tf_op jit(solution)/shard_map/ppermute | solution.py:179
  18.5 49.0 %copy-start = (bf16[640,160]{0,1:T(8,128)(2,1)S(1)}, bf16[640,160]{0,1:T(8,128)(2,1)}, u32[]{:S(2)}) copy-start(bf16[640,160]{0,1:T(8,128)(2,1)} %param.11) | copy-start | bytes 614404
  18.5 5.8 %copy-start.2 = (bf16[32,2560]{1,0:T(8,128)(2,1)}, bf16[32,2560]{1,0:T(8,128)(2,1)S(1)}, u32[]{:S(2)}) copy-start(bf16[32,2560]{1,0:T(8,128)(2,1)S(1)} %collective-permute-done.5.q1) | copy-start | bytes 491524
  18.5 24.0 %collective-permute-start.10 = (bf16[160,640]{1,0:T(8,128)(2,1)}, bf16[160,640]{1,0:T(8,128)(2,1)S(1)}, u32[]{:S(2)}, u32[]{:S(2)}) collective-permute-start(bf16[160,640]{1,0:T(8,128)(2,1)} %bitcast.93), channel_id=1, source_target_pairs={{0,4},{1,5},{2,6},{3,7},{4,0},{5,1},{6,2},{7,3},{8,12},{9,13},{10,... | collective-permute-start | bytes 614408 | tf_op jit(solution)/shard_map/ppermute | solution.py:179
  24.3 0.7 copy-start.3
  24.3 0.7 copy-start.4
  42.5 17.1 %all-to-all-start = ((bf16[16,176,128]{2,1,0:T(8,128)(2,1)}), bf16[16,176,128]{2,1,0:T(8,128)(2,1)S(1)}, u32[]{:S(2)}, u32[]{:S(2)}) async-start(bf16[16,176,128]{2,1,0:T(8,128)(2,1)} %bitcast.96), calls=%async_computation | async-start | bytes 1441792 | tf_op jit(solution)/shard_map/all_to_all | solution.py:214
  61.2 16.7 %all-to-all-start.1 = ((f32[8,88,128]{2,1,0:T(8,128)}), f32[8,88,128]{2,1,0:T(8,128)S(1)}, u32[]{:S(2)}, u32[]{:S(2)}) async-start(f32[8,88,128]{2,1,0:T(8,128)} %bitcast.21), calls=%async_computation.1 | async-start | bytes 720896 | tf_op jit(solution)/shard_map/all_to_all | solution.py:237
  67.5 7.5 %collective-permute-start.11 = (bf16[2,160,640]{2,1,0:T(8,128)(2,1)S(1)}, bf16[2,160,640]{2,1,0:T(8,128)(2,1)S(1)}, u32[]{:S(2)}, u32[]{:S(2)}) collective-permute-start(bf16[2,160,640]{2,1,0:T(8,128)(2,1)S(1)} %pad_maximum_fusion), channel_id=1, source_target_pairs={{0,1},{1,0},{2,3},{3,2},{4,5},{5,4},{6,7},{7,6},{8,9},{9,8},{10,11... | collective-permute-start | bytes 1228808 | tf_op jit(solution)/shard_map/ppermute | solution.py:179
  67.9 8.4 %collective-permute-start.12 = (bf16[2,160,640]{2,1,0:T(8,128)(2,1)S(1)}, bf16[2,160,640]{2,1,0:T(8,128)(2,1)S(1)}, u32[]{:S(2)}, u32[]{:S(2)}) collective-permute-start(bf16[2,160,640]{2,1,0:T(8,128)(2,1)S(1)} %pad_maximum_fusion), channel_id=1, source_target_pairs={{0,3},{1,2},{2,1},{3,0},{4,7},{5,6},{6,5},{7,4},{8,11},{9,10},{10,... | collective-permute-start | bytes 1228808 | tf_op jit(solution)/shard_map/ppermute | solution.py:179
  78.3 5.5 %collective-permute-start.13 = (bf16[80,128]{1,0:T(8,128)(2,1)S(1)}, bf16[80,128]{1,0:T(8,128)(2,1)S(1)}, u32[]{:S(2)}, u32[]{:S(2)}) collective-permute-start(bf16[80,128]{1,0:T(8,128)(2,1)S(1)} %divide_convert_fusion), channel_id=1, source_target_pairs={{0,8},{8,0},{16,24},{24,16},{32,40},{40,32},{48,56},{56,48},{64,72... | collective-permute-start | bytes 61448 | tf_op jit(solution)/shard_map/ppermute | solution.py:179
  83.0 11.3 %collective-permute-start.15 = (bf16[160,640]{1,0:T(8,128)(2,1)S(1)}, bf16[160,640]{1,0:T(8,128)(2,1)S(1)}, u32[]{:S(2)}, u32[]{:S(2)}) collective-permute-start(bf16[160,640]{1,0:T(8,128)(2,1)S(1)} %slice_bitcast_fusion), channel_id=1, source_target_pairs={{0,1},{1,0},{2,3},{3,2},{4,5},{5,4},{6,7},{7,6},{8,9},{9,8},{10,11... | collective-permute-start | bytes 614408 | tf_op jit(solution)/shard_map/ppermute | solution.py:179
  84.6 8.4 %all-to-all-start.2 = ((bf16[4,2,80,128]{3,2,1,0:T(8,128)(2,1)}), bf16[4,2,80,128]{3,2,1,0:T(8,128)(2,1)S(1)}, u32[]{:S(2)}, u32[]{:S(2)}) async-start(bf16[4,2,80,128]{3,2,1,0:T(8,128)(2,1)} %broadcast_in_dim.8), calls=%async_computation.2 | async-start | bytes 327680 | tf_op jit(solution)/shard_map/all_to_all | solution.py:250
  88.0 7.6 %collective-permute-start.14 = (bf16[160,640]{1,0:T(8,128)(2,1)S(1)}, bf16[160,640]{1,0:T(8,128)(2,1)S(1)}, u32[]{:S(2)}, u32[]{:S(2)}) collective-permute-start(bf16[160,640]{1,0:T(8,128)(2,1)S(1)} %slice_bitcast_fusion.1), channel_id=1, source_target_pairs={{0,3},{1,2},{2,1},{3,0},{4,7},{5,6},{6,5},{7,4},{8,11},{9,10},{10,... | collective-permute-start | bytes 614408 | tf_op jit(solution)/shard_map/ppermute | solution.py:179

commit v4 on v3

--- a/solution.py
+++ b/solution.py
@@ -15,7 +15,7 @@
 CHIPS = 16
 Y = 4
 CORE_HEADS = 4
-CHUNK = 1024
+CHUNK = 2048
 TILE = 16
 PIECE = 2 * GROUP * TILE
 STATS = 16

time: 97.1 us -> 96.4 us (level)
  no operation moved by 1% of the time
where the time goes in v4:
time: 96.4 us; the launch traced here: 95.9 us
  starting transfers between devices  39.4 us (41%)
  waiting for transfers between devices  29.8 us (31%)
  Pallas kernels  16.9 us (18%)
  local copies, waits for them, and re-layouts  4.09 us (4%)
  matrix products  2.16 us (2%)
  other arithmetic  2.08 us (2%)
  between operations  1.54 us (2%)
    ppermute x16, starting transfers between devices, swap(): return lax.ppermute(a, axis, [(i, i ^ bits) for i in range(size)])  23.4 us
    pallas_call x1, Pallas kernels, attend(): pl.pallas_call(attention_kernel, grid_spec=pltpu.PrefetchScalarGridSpec(n...  16.9 us
    ppermute x16, waiting for transfers between devices, swap(): return lax.ppermute(a, axis, [(i, i ^ bits) for i in range(size)])  13.3 us
    all_to_all x1, waiting for transfers between devices, per_device(): lax.all_to_all(out.reshape(CHIPS, PIECE + STATS, HEAD_SIZE), ('sx', 'sy')...  10.5 us
    all_to_all x1, starting transfers between devices, per_device(): lax.all_to_all(out.reshape(CHIPS, PIECE + STATS, HEAD_SIZE), ('sx', 'sy')...  6.49 us
    all_to_all x1, starting transfers between devices, per_device(): lax.all_to_all(pieces.reshape(size_y, rows + 8, HEAD_SIZE), ('sx', 'sy'),...  6.22 us
    all_to_all x1, waiting for transfers between devices, per_device(): lax.all_to_all(jnp.broadcast_to(both[None], (4, 2, rows, HEAD_SIZE)), 'sx...  4.3 us
    all_to_all x1, starting transfers between devices, per_device(): lax.all_to_all(jnp.broadcast_to(both[None], (4, 2, rows, HEAD_SIZE)), 'sx...  3.34 us
  transfers between devices with their start and end apart: 19, of which 10 were waited for; matrix products, arithmetic and copies ran while one was open for 5% of the time, Pallas kernels for 18%

profile of v4, /device:TPU:1, one launch (start us, length us, event | category | flops | bytes accessed | tf_op | source)
XLA Modules:
  0.0 95.9 jit_solution(8908194153032395454)
XLA Ops:
  0.0 3.2 %collective-permute-start = (bf16[4,5120]{1,0:T(4,128)(2,1)}, bf16[4,5120]{1,0:T(4,128)(2,1)S(1)}, u32[]{:S(2)}, u32[]{:S(2)}) collective-permute-start(bf16[4,5120]{1,0:T(4,128)(2,1)} %param.6), channel_id=1, source_target_pairs={{0,8},{8,0},{16,24},{24,16},{32,40},{40,32},{48,56},{56,48},{64,72... | collective-permute-start | bytes 122888 | tf_op jit(solution)/shard_map/ppermute | solution.py:179
  3.2 0.0 collective-permute-start.1
  3.2 1.1 %collective-permute-done = bf16[4,5120]{1,0:T(4,128)(2,1)S(1)} collective-permute-done((bf16[4,5120]{1,0:T(4,128)(2,1)}, bf16[4,5120]{1,0:T(4,128)(2,1)S(1)}, u32[]{:S(2)}, u32[]{:S(2)}) %collective-permute-start) | collective-permute-done | bytes 40992 | tf_op jit(solution)/shard_map/ppermute | solution.py:179
  4.3 0.8 broadcast_select_fusion
  5.1 0.1 fusion.11
  5.2 0.0 collective-permute-done.1
  5.3 0.4 collective-permute-start.8
  5.7 0.2 collective-permute-start.9
  5.9 1.3 %collective-permute-start.3 = (bf16[8,2560]{1,0:T(8,128)(2,1)S(1)}, bf16[8,2560]{1,0:T(8,128)(2,1)S(1)}, u32[]{:S(2)}, u32[]{:S(2)}) collective-permute-start(bf16[8,2560]{1,0:T(8,128)(2,1)S(1)} %fusion.11), channel_id=1, source_target_pairs={{0,32},{8,40},{16,48},{24,56},{32,0},{40,8},{48,16},{56,24},{64,96... | collective-permute-start | bytes 122888 | tf_op jit(solution)/shard_map/ppermute | solution.py:179
  7.1 1.4 %collective-permute-start.4 = (bf16[8,2560]{1,0:T(8,128)(2,1)S(1)}, bf16[8,2560]{1,0:T(8,128)(2,1)S(1)}, u32[]{:S(2)}, u32[]{:S(2)}) collective-permute-start(bf16[8,2560]{1,0:T(8,128)(2,1)S(1)} %fusion.11), channel_id=1, source_target_pairs={{0,48},{8,56},{16,32},{24,40},{32,16},{40,24},{48,0},{56,8},{64,11... | collective-permute-start | bytes 122888 | tf_op jit(solution)/shard_map/ppermute | solution.py:179
  8.5 0.3 collective-permute-start.2
  8.8 2.1 %collective-permute-done.3 = bf16[8,2560]{1,0:T(8,128)(2,1)S(1)} collective-permute-done((bf16[8,2560]{1,0:T(8,128)(2,1)S(1)}, bf16[8,2560]{1,0:T(8,128)(2,1)S(1)}, u32[]{:S(2)}, u32[]{:S(2)}) %collective-permute-start.3) | collective-permute-done | bytes 40992 | tf_op jit(solution)/shard_map/ppermute | solution.py:179
  10.9 0.9 collective-permute-done.4
  11.8 0.0 collective-permute-done.2
  11.9 1.3 %collective-permute-start.5 = (bf16[32,2560]{1,0:T(8,128)(2,1)S(1)}, bf16[32,2560]{1,0:T(8,128)(2,1)S(1)}, u32[]{:S(2)}, u32[]{:S(2)}) collective-permute-start(bf16[32,2560]{1,0:T(8,128)(2,1)S(1)} %pad_maximum_fusion.2.q0), channel_id=1, source_target_pairs={{0,64},{8,72},{16,80},{24,88},{32,96},{40,104},{48,112},{56,120},{... | collective-permute-start | bytes 491528 | tf_op jit(solution)/shard_map/ppermute | solution.py:179
  13.2 2.5 %collective-permute-start.6 = (bf16[32,2560]{1,0:T(8,128)(2,1)S(1)}, bf16[32,2560]{1,0:T(8,128)(2,1)S(1)}, u32[]{:S(2)}, u32[]{:S(2)}) collective-permute-start(bf16[32,2560]{1,0:T(8,128)(2,1)S(1)} %pad_maximum_fusion.2.q0), channel_id=1, source_target_pairs={{0,128},{8,136},{16,144},{24,152},{32,160},{40,168},{48,176},{56,1... | collective-permute-start | bytes 491528 | tf_op jit(solution)/shard_map/ppermute | solution.py:179
  15.6 0.2 collective-permute-start.7
  17.2 1.3 %stack.64.info = s32[10]{0:T(128)} concatenate(s32[1]{0:T(128)} %bitcast, s32[1]{0:T(128)S(6)} %copy.25, s32[1]{0:T(128)} %bitcast.2, s32[1]{0:T(128)} %bitcast.3, s32[1]{0:T(128)} %copy.24, s32[1]{0:T(128)} %collective-permute-done.1, s32[1]{0:T(128)} %bitcast.4, s32[1]{0:T(128)} %bitcast.5, s32[1]{0:T(128)} %bitcast.6, s32[1]{0:T(128)} %bitcast.7), dimensions={0} | concatenate | bytes 80 | tf_op jit(solution)/shard_map/stack | solution.py:201
  18.5 0.0 collective-permute-done.5.q1
  18.5 5.8 %collective-permute-start.10 = (bf16[160,640]{1,0:T(8,128)(2,1)}, bf16[160,640]{1,0:T(8,128)(2,1)S(1)}, u32[]{:S(2)}, u32[]{:S(2)}) collective-permute-start(bf16[160,640]{1,0:T(8,128)(2,1)} %bitcast.93), channel_id=1, source_target_pairs={{0,4},{1,5},{2,6},{3,7},{4,0},{5,1},{6,2},{7,3},{8,12},{9,13},{10,... | collective-permute-start | bytes 614408 | tf_op jit(solution)/shard_map/ppermute | solution.py:179
  24.2 0.0 collective-permute-done.6.q2
  24.3 0.0 collective-permute-done.7.q3
  24.3 0.0 collective-permute-done.8.key_pair
  24.3 0.6 copy-done.3
  24.9 0.1 copy-done.4
  25.0 16.9 %shard_map.64 = bf16[4,4,176,128]{3,2,1,0:T(8,128)(2,1)} custom-call(s32[10]{0:T(128)} %stack.64.info, bf16[32,2560]{1,0:T(8,128)(2,1)} %copy-done.1, bf16[32,2560]{1,0:T(8,128)(2,1)} %copy-done.2, bf16[32,2560]{1,0:T(8,128)(2,1)} %copy-done.3, bf16[32,2560]{1,0:T(8,128)(2,1)} %copy-done.4, bf16[2048,1024]{1,0:T(8,128)(2,1)} %key_own, ...), custom_call_target="tpu_custom_call" | custom-call | flops 10737418240 | bytes 8388608 | tf_op jit(solution)/shard_map/pallas_call | solution.py:130
  41.8 6.5 %all-to-all-start = ((bf16[16,176,128]{2,1,0:T(8,128)(2,1)}), bf16[16,176,128]{2,1,0:T(8,128)(2,1)S(1)}, u32[]{:S(2)}, u32[]{:S(2)}) async-start(bf16[16,176,128]{2,1,0:T(8,128)(2,1)} %bitcast.96), calls=%async_computation | async-start | bytes 1441792 | tf_op jit(solution)/shard_map/all_to_all | solution.py:214
  48.4 0.1 pad.16.clone
  48.4 10.5 %all-to-all-done = bf16[16,176,128]{2,1,0:T(8,128)(2,1)S(1)} async-done(((bf16[16,176,128]{2,1,0:T(8,128)(2,1)}), bf16[16,176,128]{2,1,0:T(8,128)(2,1)S(1)}, u32[]{:S(2)}, u32[]{:S(2)}) %all-to-all-start) | async-done | bytes 720928 | tf_op jit(solution)/shard_map/all_to_all | solution.py:214
  58.9 0.2 fusion.34
  59.1 0.1 reshape.66
  59.2 0.4 multiply_reduce_fusion
  59.6 0.1 reshape.67
  59.7 0.1 fusion.8
  59.8 0.8 broadcast_in_dim.7
  60.6 6.2 %all-to-all-start.1 = ((f32[8,88,128]{2,1,0:T(8,128)}), f32[8,88,128]{2,1,0:T(8,128)S(1)}, u32[]{:S(2)}, u32[]{:S(2)}) async-start(f32[8,88,128]{2,1,0:T(8,128)} %bitcast.21), calls=%async_computation.1 | async-start | bytes 720896 | tf_op jit(solution)/shard_map/all_to_all | solution.py:237
  66.8 0.4 collective-permute-start.11
  67.2 0.8 collective-permute-start.12
  68.0 6.4 %collective-permute-done.11 = bf16[2,160,640]{2,1,0:T(8,128)(2,1)S(1)} collective-permute-done((bf16[2,160,640]{2,1,0:T(8,128)(2,1)S(1)}, bf16[2,160,640]{2,1,0:T(8,128)(2,1)S(1)}, u32[]{:S(2)}, u32[]{:S(2)}) %collective-permute-start.11) | collective-permute-done | bytes 409632 | tf_op jit(solution)/shard_map/ppermute | solution.py:179
  74.4 1.2 %collective-permute-done.12 = bf16[2,160,640]{2,1,0:T(8,128)(2,1)S(1)} collective-permute-done((bf16[2,160,640]{2,1,0:T(8,128)(2,1)S(1)}, bf16[2,160,640]{2,1,0:T(8,128)(2,1)S(1)}, u32[]{:S(2)}, u32[]{:S(2)}) %collective-permute-start.12) | collective-permute-done | bytes 409632 | tf_op jit(solution)/shard_map/ppermute | solution.py:179
  75.6 1.7 %all-to-all-done.1 = f32[8,88,128]{2,1,0:T(8,128)S(1)} async-done(((f32[8,88,128]{2,1,0:T(8,128)}), f32[8,88,128]{2,1,0:T(8,128)S(1)}, u32[]{:S(2)}, u32[]{:S(2)}) %all-to-all-start.1) | async-done | bytes 360480 | tf_op jit(solution)/shard_map/all_to_all | solution.py:237
  77.3 0.1 copy.18
  77.4 0.2 multiply_reduce_fusion.1
  77.6 0.1 divide_convert_fusion
  77.7 4.6 %collective-permute-start.13 = (bf16[80,128]{1,0:T(8,128)(2,1)S(1)}, bf16[80,128]{1,0:T(8,128)(2,1)S(1)}, u32[]{:S(2)}, u32[]{:S(2)}) collective-permute-start(bf16[80,128]{1,0:T(8,128)(2,1)S(1)} %divide_convert_fusion), channel_id=1, source_target_pairs={{0,8},{8,0},{16,24},{24,16},{32,40},{40,32},{48,56},{56,48},{64,72... | collective-permute-start | bytes 61448 | tf_op jit(solution)/shard_map/ppermute | solution.py:179
  82.3 0.4 collective-permute-start.15
  82.7 0.5 collective-permute-done.13
  83.1 0.1 select_bitcast_fusion.1
  83.3 0.7 broadcast_in_dim.8
  83.9 3.3 %all-to-all-start.2 = ((bf16[4,2,80,128]{3,2,1,0:T(8,128)(2,1)}), bf16[4,2,80,128]{3,2,1,0:T(8,128)(2,1)S(1)}, u32[]{:S(2)}, u32[]{:S(2)}) async-start(bf16[4,2,80,128]{3,2,1,0:T(8,128)(2,1)} %broadcast_in_dim.8), calls=%async_computation.2 | async-start | bytes 327680 | tf_op jit(solution)/shard_map/all_to_all | solution.py:250
  87.3 0.7 collective-permute-start.14
  88.0 4.3 %all-to-all-done.2 = bf16[4,2,80,128]{3,2,1,0:T(8,128)(2,1)S(1)} async-done(((bf16[4,2,80,128]{3,2,1,0:T(8,128)(2,1)}), bf16[4,2,80,128]{3,2,1,0:T(8,128)(2,1)S(1)}, u32[]{:S(2)}, u32[]{:S(2)}) %all-to-all-start.2) | async-done | bytes 163872 | tf_op jit(solution)/shard_map/all_to_all | solution.py:250
  92.4 0.1 copy.19
  92.4 0.2 reshape.70
  92.6 0.1 fusion.20
  92.8 0.2 convolution_add_fusion.4
  93.0 0.2 convolution_add_fusion.3
  93.2 0.2 convolution_add_fusion.2
  93.4 0.2 fusion.3
  93.6 0.0 collective-permute-done.15
  93.6 0.2 fusion.14
  93.8 1.1 %collective-permute-done.14 = bf16[160,640]{1,0:T(8,128)(2,1)S(1)} collective-permute-done((bf16[160,640]{1,0:T(8,128)(2,1)S(1)}, bf16[160,640]{1,0:T(8,128)(2,1)S(1)}, u32[]{:S(2)}, u32[]{:S(2)}) %collective-permute-start.14) | collective-permute-done | bytes 204832 | tf_op jit(solution)/shard_map/ppermute | solution.py:179
  94.9 0.1 fusion.1
  95.1 0.9 fusion.2
  (25 shorter events, 0.3 us)
Async XLA Ops:
  0.0 4.3 %collective-permute-start = (bf16[4,5120]{1,0:T(4,128)(2,1)}, bf16[4,5120]{1,0:T(4,128)(2,1)S(1)}, u32[]{:S(2)}, u32[]{:S(2)}) collective-permute-start(bf16[4,5120]{1,0:T(4,128)(2,1)} %param.6), channel_id=1, source_target_pairs={{0,8},{8,0},{16,24},{24,16},{32,40},{40,32},{48,56},{56,48},{64,72... | collective-permute-start | bytes 122888 | tf_op jit(solution)/shard_map/ppermute | solution.py:179
  3.2 2.0 %collective-permute-start.1 = (s32[1]{0:T(128)}, s32[1]{0:T(128)}, u32[]{:S(2)}, u32[]{:S(2)}) collective-permute-start(s32[1]{0:T(128)} %param.10), channel_id=1, source_target_pairs={{0,8},{8,0},{16,24},{24,16},{32,40},{40,32},{48,56},{56,48},{64,72... | collective-permute-start | bytes 20 | tf_op jit(solution)/shard_map/ppermute | solution.py:179
  5.3 19.0 %collective-permute-start.8 = (bf16[2048,1024]{1,0:T(8,128)(2,1)}, bf16[2048,1024]{1,0:T(8,128)(2,1)}, u32[]{:S(2)}, u32[]{:S(2)}) collective-permute-start(bf16[2048,1024]{1,0:T(8,128)(2,1)} %key_own), channel_id=1, source_target_pairs={{0,8},{8,0},{16,24},{24,16},{32,40},{40,32},{48,56},{56,48},{64,72... | collective-permute-start | bytes 12582920 | tf_op jit(solution)/shard_map/ppermute | solution.py:179
  5.7 18.6 %collective-permute-start.9 = (bf16[2048,1024]{1,0:T(8,128)(2,1)}, bf16[2048,1024]{1,0:T(8,128)(2,1)}, u32[]{:S(2)}, u32[]{:S(2)}) collective-permute-start(bf16[2048,1024]{1,0:T(8,128)(2,1)} %value_own), channel_id=1, source_target_pairs={{0,8},{8,0},{16,24},{24,16},{32,40},{40,32},{48,56},{56,48},{64,72... | collective-permute-start | bytes 12582920 | tf_op jit(solution)/shard_map/ppermute | solution.py:179
  5.9 5.0 %collective-permute-start.3 = (bf16[8,2560]{1,0:T(8,128)(2,1)S(1)}, bf16[8,2560]{1,0:T(8,128)(2,1)S(1)}, u32[]{:S(2)}, u32[]{:S(2)}) collective-permute-start(bf16[8,2560]{1,0:T(8,128)(2,1)S(1)} %fusion.11), channel_id=1, source_target_pairs={{0,32},{8,40},{16,48},{24,56},{32,0},{40,8},{48,16},{56,24},{64,96... | collective-permute-start | bytes 122888 | tf_op jit(solution)/shard_map/ppermute | solution.py:179
  7.1 4.7 %collective-permute-start.4 = (bf16[8,2560]{1,0:T(8,128)(2,1)S(1)}, bf16[8,2560]{1,0:T(8,128)(2,1)S(1)}, u32[]{:S(2)}, u32[]{:S(2)}) collective-permute-start(bf16[8,2560]{1,0:T(8,128)(2,1)S(1)} %fusion.11), channel_id=1, source_target_pairs={{0,48},{8,56},{16,32},{24,40},{32,16},{40,24},{48,0},{56,8},{64,11... | collective-permute-start | bytes 122888 | tf_op jit(solution)/shard_map/ppermute | solution.py:179
  8.5 3.3 %collective-permute-start.2 = (bf16[8,2560]{1,0:T(8,128)(2,1)S(1)}, bf16[8,2560]{1,0:T(8,128)(2,1)S(1)}, u32[]{:S(2)}, u32[]{:S(2)}) collective-permute-start(bf16[8,2560]{1,0:T(8,128)(2,1)S(1)} %fusion.11), channel_id=1, source_target_pairs={{0,16},{8,24},{16,0},{24,8},{32,48},{40,56},{48,32},{56,40},{64,80... | collective-permute-start | bytes 122888 | tf_op jit(solution)/shard_map/ppermute | solution.py:179
  11.9 12.4 %copy-start.1 = (bf16[32,2560]{1,0:T(8,128)(2,1)}, bf16[32,2560]{1,0:T(8,128)(2,1)S(1)}, u32[]{:S(2)}) copy-start(bf16[32,2560]{1,0:T(8,128)(2,1)S(1)} %pad_maximum_fusion.2.q0) | copy-start | bytes 491524
  11.9 6.6 %collective-permute-start.5 = (bf16[32,2560]{1,0:T(8,128)(2,1)S(1)}, bf16[32,2560]{1,0:T(8,128)(2,1)S(1)}, u32[]{:S(2)}, u32[]{:S(2)}) collective-permute-start(bf16[32,2560]{1,0:T(8,128)(2,1)S(1)} %pad_maximum_fusion.2.q0), channel_id=1, source_target_pairs={{0,64},{8,72},{16,80},{24,88},{32,96},{40,104},{48,112},{56,120},{... | collective-permute-start | bytes 491528 | tf_op jit(solution)/shard_map/ppermute | solution.py:179
  13.2 11.1 %collective-permute-start.6 = (bf16[32,2560]{1,0:T(8,128)(2,1)S(1)}, bf16[32,2560]{1,0:T(8,128)(2,1)S(1)}, u32[]{:S(2)}, u32[]{:S(2)}) collective-permute-start(bf16[32,2560]{1,0:T(8,128)(2,1)S(1)} %pad_maximum_fusion.2.q0), channel_id=1, source_target_pairs={{0,128},{8,136},{16,144},{24,152},{32,160},{40,168},{48,176},{56,1... | collective-permute-start | bytes 491528 | tf_op jit(solution)/shard_map/ppermute | solution.py:179
  15.6 8.7 %collective-permute-start.7 = (bf16[32,2560]{1,0:T(8,128)(2,1)S(1)}, bf16[32,2560]{1,0:T(8,128)(2,1)S(1)}, u32[]{:S(2)}, u32[]{:S(2)}) collective-permute-start(bf16[32,2560]{1,0:T(8,128)(2,1)S(1)} %pad_maximum_fusion.2.q0), channel_id=1, source_target_pairs={{0,192},{8,200},{16,208},{24,216},{32,224},{40,232},{48,240},{56,2... | collective-permute-start | bytes 491528 | tf_op jit(solution)/shard_map/ppermute | solution.py:179
  18.5 48.3 %copy-start = (bf16[640,160]{0,1:T(8,128)(2,1)S(1)}, bf16[640,160]{0,1:T(8,128)(2,1)}, u32[]{:S(2)}) copy-start(bf16[640,160]{0,1:T(8,128)(2,1)} %param.11) | copy-start | bytes 614404
  18.5 5.8 %copy-start.2 = (bf16[32,2560]{1,0:T(8,128)(2,1)}, bf16[32,2560]{1,0:T(8,128)(2,1)S(1)}, u32[]{:S(2)}) copy-start(bf16[32,2560]{1,0:T(8,128)(2,1)S(1)} %collective-permute-done.5.q1) | copy-start | bytes 491524
  18.5 23.4 %collective-permute-start.10 = (bf16[160,640]{1,0:T(8,128)(2,1)}, bf16[160,640]{1,0:T(8,128)(2,1)S(1)}, u32[]{:S(2)}, u32[]{:S(2)}) collective-permute-start(bf16[160,640]{1,0:T(8,128)(2,1)} %bitcast.93), channel_id=1, source_target_pairs={{0,4},{1,5},{2,6},{3,7},{4,0},{5,1},{6,2},{7,3},{8,12},{9,13},{10,... | collective-permute-start | bytes 614408 | tf_op jit(solution)/shard_map/ppermute | solution.py:179
  24.3 0.7 copy-start.3
  24.3 0.7 copy-start.4
  41.8 17.1 %all-to-all-start = ((bf16[16,176,128]{2,1,0:T(8,128)(2,1)}), bf16[16,176,128]{2,1,0:T(8,128)(2,1)S(1)}, u32[]{:S(2)}, u32[]{:S(2)}) async-start(bf16[16,176,128]{2,1,0:T(8,128)(2,1)} %bitcast.96), calls=%async_computation | async-start | bytes 1441792 | tf_op jit(solution)/shard_map/all_to_all | solution.py:214
  60.6 16.7 %all-to-all-start.1 = ((f32[8,88,128]{2,1,0:T(8,128)}), f32[8,88,128]{2,1,0:T(8,128)S(1)}, u32[]{:S(2)}, u32[]{:S(2)}) async-start(f32[8,88,128]{2,1,0:T(8,128)} %bitcast.21), calls=%async_computation.1 | async-start | bytes 720896 | tf_op jit(solution)/shard_map/all_to_all | solution.py:237
  66.8 7.5 %collective-permute-start.11 = (bf16[2,160,640]{2,1,0:T(8,128)(2,1)S(1)}, bf16[2,160,640]{2,1,0:T(8,128)(2,1)S(1)}, u32[]{:S(2)}, u32[]{:S(2)}) collective-permute-start(bf16[2,160,640]{2,1,0:T(8,128)(2,1)S(1)} %pad_maximum_fusion), channel_id=1, source_target_pairs={{0,1},{1,0},{2,3},{3,2},{4,5},{5,4},{6,7},{7,6},{8,9},{9,8},{10,11... | collective-permute-start | bytes 1228808 | tf_op jit(solution)/shard_map/ppermute | solution.py:179
  67.2 8.4 %collective-permute-start.12 = (bf16[2,160,640]{2,1,0:T(8,128)(2,1)S(1)}, bf16[2,160,640]{2,1,0:T(8,128)(2,1)S(1)}, u32[]{:S(2)}, u32[]{:S(2)}) collective-permute-start(bf16[2,160,640]{2,1,0:T(8,128)(2,1)S(1)} %pad_maximum_fusion), channel_id=1, source_target_pairs={{0,3},{1,2},{2,1},{3,0},{4,7},{5,6},{6,5},{7,4},{8,11},{9,10},{10,... | collective-permute-start | bytes 1228808 | tf_op jit(solution)/shard_map/ppermute | solution.py:179
  77.7 5.5 %collective-permute-start.13 = (bf16[80,128]{1,0:T(8,128)(2,1)S(1)}, bf16[80,128]{1,0:T(8,128)(2,1)S(1)}, u32[]{:S(2)}, u32[]{:S(2)}) collective-permute-start(bf16[80,128]{1,0:T(8,128)(2,1)S(1)} %divide_convert_fusion), channel_id=1, source_target_pairs={{0,8},{8,0},{16,24},{24,16},{32,40},{40,32},{48,56},{56,48},{64,72... | collective-permute-start | bytes 61448 | tf_op jit(solution)/shard_map/ppermute | solution.py:179
  82.3 11.3 %collective-permute-start.15 = (bf16[160,640]{1,0:T(8,128)(2,1)S(1)}, bf16[160,640]{1,0:T(8,128)(2,1)S(1)}, u32[]{:S(2)}, u32[]{:S(2)}) collective-permute-start(bf16[160,640]{1,0:T(8,128)(2,1)S(1)} %slice_bitcast_fusion), channel_id=1, source_target_pairs={{0,1},{1,0},{2,3},{3,2},{4,5},{5,4},{6,7},{7,6},{8,9},{9,8},{10,11... | collective-permute-start | bytes 614408 | tf_op jit(solution)/shard_map/ppermute | solution.py:179
  83.9 8.4 %all-to-all-start.2 = ((bf16[4,2,80,128]{3,2,1,0:T(8,128)(2,1)}), bf16[4,2,80,128]{3,2,1,0:T(8,128)(2,1)S(1)}, u32[]{:S(2)}, u32[]{:S(2)}) async-start(bf16[4,2,80,128]{3,2,1,0:T(8,128)(2,1)} %broadcast_in_dim.8), calls=%async_computation.2 | async-start | bytes 327680 | tf_op jit(solution)/shard_map/all_to_all | solution.py:250
  87.3 7.6 %collective-permute-start.14 = (bf16[160,640]{1,0:T(8,128)(2,1)S(1)}, bf16[160,640]{1,0:T(8,128)(2,1)S(1)}, u32[]{:S(2)}, u32[]{:S(2)}) collective-permute-start(bf16[160,640]{1,0:T(8,128)(2,1)S(1)} %slice_bitcast_fusion.1), channel_id=1, source_target_pairs={{0,3},{1,2},{2,1},{3,0},{4,7},{5,6},{6,5},{7,4},{8,11},{9,10},{10,... | collective-permute-start | bytes 614408 | tf_op jit(solution)/shard_map/ppermute | solution.py:179
